TPU v7x, 256 devices: a whole 4x4x8 slice. The times are simulated.
256 devices in a mesh: row: 8 (over x, core), col: 32 (over z, y).
Axes of the slice: x: 4, y: 4, z: 8, core: 2. Of those that a mesh axis runs over, the one named last changes fastest.
Arguments:
- tokens: bfloat16 [1024, 4096], P('row', 'col'), may hold values from -6 to 6
- gate_weight: bfloat16 [4096, 16384], P('row', 'col'), may hold values from -0.09375 to 0.09375
- up_weight: bfloat16 [4096, 16384], P('row', 'col'), may hold values from -0.09375 to 0.09375
- down_weight: bfloat16 [16384, 4096], P('row', 'col'), may hold values from -0.046875 to 0.046875
- out_grad: bfloat16 [1024, 4096], P('row', 'col'), may hold values from -6 to 6
Outputs:
- output: bfloat16 [1024, 4096], P('row', 'col')
- token_grad: bfloat16 [1024, 4096], P('row', 'col')
- gate_grad: bfloat16 [4096, 16384], P('row', 'col')
- up_grad: bfloat16 [4096, 16384], P('row', 'col')
- down_grad: bfloat16 [16384, 4096], P('row', 'col')
All inputs are finite; a program needn't handle non-finite values.
Results may differ from a plain program's by a relative error of at most 0.005.
Values may be sent and summed in bfloat16 or wider, within the bound.
A program may use at most 128 MiB of HBM per device.

v0:
```python
import jax
import jax.numpy as jnp
from jax import lax
from jax.sharding import PartitionSpec as P


def tdot(left, right):
    return lax.dot_general(
        left, right, (((0,), (0,)), ((), ())), preferred_element_type=jnp.float32
    )


def rdot(left, right):
    return lax.dot_general(
        left, right, (((1,), (1,)), ((), ())), preferred_element_type=jnp.float32
    )


def local(tokens, gate_weight, up_weight, down_weight, out_grad):
    token_full, cotan_full = (
        lax.all_gather(tokens, "col", axis=1, tiled=True),
        lax.all_gather(out_grad, "col", axis=1, tiled=True),
    )
    gate_cols, up_cols, down_cols = (
        lax.all_gather(gate_weight, "row", axis=0, tiled=True),
        lax.all_gather(up_weight, "row", axis=0, tiled=True),
        lax.all_gather(down_weight, "row", axis=0, tiled=True),
    )
    gate_proj = jnp.dot(token_full, gate_cols, preferred_element_type=jnp.float32)
    up_proj = jnp.dot(token_full, up_cols, preferred_element_type=jnp.float32)
    swish_out = jax.nn.silu(gate_proj)
    hidden = (swish_out * up_proj).astype(jnp.bfloat16)
    hidden_full = lax.all_gather(hidden, "col", axis=1, tiled=True)
    output = jnp.dot(hidden_full, down_cols, preferred_element_type=jnp.float32).astype(
        jnp.bfloat16
    )
    partial_hidden = rdot(out_grad, down_cols)
    grad_hidden = lax.psum_scatter(partial_hidden, "col", scatter_dimension=1, tiled=True)
    sigmoid_g = jax.nn.sigmoid(gate_proj)
    grad_gate = (grad_hidden * up_proj * sigmoid_g * (1.0 + gate_proj * (1.0 - sigmoid_g))).astype(
        jnp.bfloat16
    )
    grad_up = (grad_hidden * swish_out).astype(jnp.bfloat16)
    partial_input = rdot(grad_gate, gate_cols) + rdot(grad_up, up_cols)
    token_grad = lax.psum_scatter(partial_input, "col", scatter_dimension=1, tiled=True).astype(
        jnp.bfloat16
    )
    token_panel, hidden_panel = (
        lax.all_to_all(token_full, "row", split_axis=1, concat_axis=0, tiled=True),
        lax.all_to_all(hidden_full, "row", split_axis=1, concat_axis=0, tiled=True),
    )
    cot_piece = lax.all_gather(out_grad, "row", axis=0, tiled=True)
    gate_piece = lax.all_gather(grad_gate, "row", axis=0, tiled=True)
    up_piece = lax.all_gather(grad_up, "row", axis=0, tiled=True)
    gate_sum = tdot(token_panel, gate_piece)
    up_sum = tdot(token_panel, up_piece)
    down_sum = tdot(hidden_panel, cot_piece)
    return (
        output,
        token_grad,
        gate_sum.astype(jnp.bfloat16),
        up_sum.astype(jnp.bfloat16),
        down_sum.astype(jnp.bfloat16),
    )


def solution(mesh):
    placed = (P("row", "col"), P("row", "col"), P("row", "col"), P("row", "col"), P("row", "col"))
    return jax.shard_map(
        local,
        mesh=mesh,
        in_specs=placed,
        out_specs=(
            P("row", "col"),
            P("row", "col"),
            P("row", "col"),
            P("row", "col"),
            P("row", "col"),
        ),
        check_vma=False,
    )
```

profile of v0, /device:TPU:4, one launch (start us, length us, event | category | flops | bytes accessed | tf_op | source)
XLA Modules:
  0.0 822.6 jit_solution(4823125549215602209)
XLA Ops:
  7.2 0.0 all-gather.16.cloned.1.call-start
  7.2 0.7 all-gather.16.cloned.1.call-update
  7.9 0.0 all-gather.8.cloned.1.call-start
  7.9 1.5 copy.15
  9.4 0.0 all-gather.8.cloned.1.call-update
  9.4 0.0 all-gather.12.cloned.1.call-start
  9.5 0.7 all-gather.12.cloned.1.call-update
  10.2 0.0 all-gather.10.cloned.1.call-start
  10.2 0.5 all-gather.10.cloned.1.call-update
  10.8 0.0 reduce-scatter.3.cloned.1.call-start
  10.8 35.4 %all-gather.16.cloned.1.call-done = bf16[16384,128]{1,0:T(8,128)(2,1)} async-done(((bf16[2048,128]{1,0:T(8,128)(2,1)}), bf16[16384,128]{1,0:T(8,128)(2,1)}) %all-gather.16.cloned.1.call-update) | async-done | bytes 4194320 | tf_op jit(solution)/shard_map/all_gather | solution.py:27
  46.2 6.7 fusion.4
  52.9 0.0 reduce-scatter.3.cloned.1.call-update
  52.9 0.0 all-gather.14.cloned.1.call-start
  53.0 73.9 %all-gather.8.cloned.1.call-done = bf16[128,4096]{0,1:T(8,128)(2,1)} async-done(((bf16[128,128]{0,1:T(8,128)(2,1)}), bf16[128,4096]{0,1:T(8,128)(2,1)}) %all-gather.8.cloned.1.call-update) | async-done | bytes 1048592 | tf_op jit(solution)/shard_map/all_gather | solution.py:21
  126.9 32.9 %all-gather.12.cloned.1.call-done = bf16[4096,512]{1,0:T(8,128)(2,1)} async-done(((bf16[512,512]{1,0:T(8,128)(2,1)}), bf16[4096,512]{1,0:T(8,128)(2,1)}) %all-gather.12.cloned.1.call-update) | async-done | bytes 4194320 | tf_op jit(solution)/shard_map/all_gather | solution.py:26
  159.7 3.3 fusion.3
  163.0 33.1 %all-gather.10.cloned.1.call-done = bf16[4096,512]{1,0:T(8,128)(2,1)} async-done(((bf16[512,512]{1,0:T(8,128)(2,1)}), bf16[4096,512]{1,0:T(8,128)(2,1)}) %all-gather.10.cloned.1.call-update) | async-done | bytes 4194320 | tf_op jit(solution)/shard_map/all_gather | solution.py:25
  196.1 234.4 %reduce-scatter.3.cloned.1.call-done = f32[128,512]{1,0:T(8,128)} async-done(((f32[128,16384]{1,0:T(8,128)}), f32[128,512]{1,0:T(8,128)}) %reduce-scatter.3.cloned.1.call-update) | async-done | bytes 262160 | tf_op jit(solution)/shard_map/reduce_scatter | solution.py:38
  430.5 4.1 multiply_convert_fusion
  434.7 0.0 copy-start.1
  434.7 0.0 all-gather.14.cloned.1.call-update
  434.7 0.0 all-gather.18.cloned.1.call-start
  434.7 0.7 all-gather.18.cloned.1.call-update
  435.4 0.0 all-gather.20.cloned.1.call-start
  435.5 0.7 all-gather.20.cloned.1.call-update
  436.2 0.0 reduce-scatter.5.cloned.1.call-start
  436.2 0.0 copy-start
  436.2 3.9 fusion.5
  440.1 0.0 copy-done.1
  440.1 0.0 copy-done
  440.1 2.8 convolution_add_fusion
  443.0 0.0 reduce-scatter.5.cloned.1.call-update
  443.0 4.8 all-to-all-start
  447.8 68.6 %all-gather.14.cloned.1.call-done = bf16[128,16384]{1,0:T(8,128)(2,1)} async-done(((bf16[128,512]{1,0:T(8,128)(2,1)}), bf16[128,16384]{1,0:T(8,128)(2,1)}) %all-gather.14.cloned.1.call-update) | async-done | bytes 4194320 | tf_op jit(solution)/shard_map/all_gather | solution.py:33
  516.4 4.8 copy.22
  521.2 0.0 all-to-all-done
  521.2 0.0 copy-start.2
  521.2 5.2 all-to-all-start.1
  526.4 0.0 copy-done.2
  526.4 62.1 %all_gather.31 = bf16[1024,128]{1,0:T(8,128)(2,1)S(1)} all-gather(bf16[128,128]{1,0:T(8,128)(2,1)S(1)} %copy-done.2), channel_id=1, replica_groups=mesh['row'=8,'col'=32] {'row'}, dimensions={0}, use_global_device_ids=true | all-gather | bytes 294912 | tf_op jit(solution)/shard_map/all_gather | solution.py:52
  588.5 0.5 copy.16
  589.1 0.0 all-gather.18.cloned.1.call-done
  589.1 2.0 fusion
  591.0 1.0 copy.18
  592.1 0.0 all-gather.20.cloned.1.call-done
  592.1 2.0 fusion.1
  594.0 1.0 copy.19
  595.0 210.0 %reduce-scatter.5.cloned.1.call-done = f32[128,128]{1,0:T(8,128)} async-done(((f32[128,4096]{1,0:T(8,128)}), f32[128,128]{1,0:T(8,128)}) %reduce-scatter.5.cloned.1.call-update) | async-done | bytes 65552 | tf_op jit(solution)/shard_map/reduce_scatter | solution.py:45
  805.0 1.5 convert_element_type.34
  806.5 5.3 convolution_convert_fusion.3
  811.8 0.0 all-to-all-done.1
  811.8 4.3 convolution_convert_fusion
Async XLA Ops:
  7.2 39.0 %all-gather.16.cloned.1.call-start = ((), (), s32[]{:S(2)}) async-start(), calls=%async_computation.8 | async-start | bytes 4718592 | tf_op jit(solution)/shard_map/all_gather | solution.py:27
  7.9 119.0 %all-gather.8.cloned.1.call-start = ((), (), s32[]{:S(2)}) async-start(), calls=%async_computation.4 | async-start | bytes 1081344 | tf_op jit(solution)/shard_map/all_gather | solution.py:21
  9.4 150.3 %all-gather.12.cloned.1.call-start = ((), (), s32[]{:S(2)}) async-start(), calls=%async_computation.6 | async-start | bytes 4718592 | tf_op jit(solution)/shard_map/all_gather | solution.py:26
  10.2 185.9 %all-gather.10.cloned.1.call-start = ((), (), s32[]{:S(2)}) async-start(), calls=%async_computation.5 | async-start | bytes 4718592 | tf_op jit(solution)/shard_map/all_gather | solution.py:25
  10.8 419.8 %reduce-scatter.3.cloned.1.call-start = ((), (), s32[]{:S(2)}) async-start(), calls=%async_computation.9 | async-start | bytes 8650752 | tf_op jit(solution)/shard_map/reduce_scatter | solution.py:38
  52.9 463.5 %all-gather.14.cloned.1.call-start = ((), (), s32[]{:S(2)}) async-start(), calls=%async_computation.7 | async-start | bytes 4325376 | tf_op jit(solution)/shard_map/all_gather | solution.py:33
  434.7 5.5 copy-start.1
  434.7 154.4 %all-gather.18.cloned.1.call-start = ((), (), s32[]{:S(2)}) async-start(), calls=%async_computation.11 | async-start | bytes 1179648 | tf_op jit(solution)/shard_map/all_gather | solution.py:53
  435.4 156.6 %all-gather.20.cloned.1.call-start = ((), (), s32[]{:S(2)}) async-start(), calls=%async_computation.12 | async-start | bytes 1179648 | tf_op jit(solution)/shard_map/all_gather | solution.py:54
  436.2 368.8 %reduce-scatter.5.cloned.1.call-start = ((), (), s32[]{:S(2)}) async-start(), calls=%async_computation.10 | async-start | bytes 2162688 | tf_op jit(solution)/shard_map/reduce_scatter | solution.py:45
  436.2 3.9 copy-start
  443.0 78.2 %all-to-all-start = ((bf16[128,8,512]{0,2,1:T(8,128)(2,1)}), bf16[128,8,512]{0,2,1:T(8,128)(2,1)S(1)}, u32[]{:S(2)}, u32[]{:S(2)}) async-start(bf16[128,8,512]{0,2,1:T(8,128)(2,1)} %bitcast), calls=%async_computation.2 | async-start | bytes 2097152 | tf_op jit(solution)/shard_map/all_to_all | solution.py:49
  521.2 5.2 copy-start.2
  521.2 290.6 %all-to-all-start.1 = ((bf16[128,8,2048]{2,0,1:T(8,128)(2,1)}), bf16[128,8,2048]{2,0,1:T(8,128)(2,1)}, u32[]{:S(2)}, u32[]{:S(2)}) async-start(bf16[128,8,2048]{2,0,1:T(8,128)(2,1)} %bitcast.33), calls=%async_computation.3 | async-start | bytes 8388608 | tf_op jit(solution)/shard_map/all_to_all | solution.py:50
Sparse Core Ops, SparseCore 0:
  9.9 36.2 all-gather.15
  49.3 77.4 all-gather.7
  128.7 30.9 all-gather.11
  161.4 34.6 all-gather.9
  200.0 230.4 reduce-scatter.2
  434.8 81.5 all-gather.13
  519.0 28.7 all-gather.17
  550.4 32.7 all-gather.19
  587.5 217.4 reduce-scatter.4
where the time goes:
time: 823 us
  waiting for transfers between devices  692 us (84%)
  blocking collectives  62.1 us (8%)
  matrix products  34.3 us (4%)
  between operations  13.9 us (2%)
  starting transfers between devices  10.3 us (1%)
  local copies, waits for them, and re-layouts  8.82 us (1%)
    reduce_scatter x1, waiting for transfers between devices, local(): lax.psum_scatter(partial_hidden, 'col', scatter_dimension=1, tiled=True)  234 us
    reduce_scatter x1, waiting for transfers between devices, local(): lax.psum_scatter(partial_input, 'col', scatter_dimension=1, tiled=True)  210 us
    all_gather x1, waiting for transfers between devices, local(): lax.all_gather(tokens, 'col', axis=1, tiled=True)  73.9 us
    all_gather x1, waiting for transfers between devices, local(): hidden_full = lax.all_gather(hidden, 'col', axis=1, tiled=True)  68.6 us
    all_gather x1, blocking collectives, local(): cot_piece = lax.all_gather(out_grad, 'row', axis=0, tiled=True)  62.1 us
    all_gather x1, waiting for transfers between devices, local(): lax.all_gather(down_weight, 'row', axis=0, tiled=True)  35.4 us
    all_gather x1, waiting for transfers between devices, local(): lax.all_gather(gate_weight, 'row', axis=0, tiled=True)  33.1 us
    all_gather x1, waiting for transfers between devices, local(): lax.all_gather(up_weight, 'row', axis=0, tiled=True)  32.9 us
  transfers between devices with their start and end apart: 11, of which 7 were waited for; matrix products, arithmetic and copies ran while one was open for 4% of the time, Pallas kernels for 0%

commit v1 on v0

v1 whole, which is shorter than its diff:
```python
import functools

import jax
import jax.numpy as jnp
from jax import lax
from jax.experimental import pallas as pl
from jax.experimental.pallas import tpu as pltpu
from jax.sharding import PartitionSpec as P

MESH = pl.DeviceIdType.MESH
BF = jnp.bfloat16
F32 = jnp.float32


def nn(a, b):
    return lax.dot_general(a, b, (((1,), (0,)), ((), ())), preferred_element_type=F32)


def nt(a, b):
    return lax.dot_general(a, b, (((1,), (1,)), ((), ())), preferred_element_type=F32)


def tn(a, b):
    return lax.dot_general(a, b, (((0,), (0,)), ((), ())), preferred_element_type=F32)


def kernel(
    dims,
    tok, cot, gate_hbm, up_hbm, down,
    out_o, tg_o, gg_o, ug_o, dg_o,
    xg, gw, dp, hid,
    acc_a, ms_a, mr_a, xs_a, xr_a,
    acc_b, ms_b, mr_b, xs_b, xr_b,
    o32, os, oown, yr, zs, zr, zown, fs, dgs,
    t1s, t1r, tds, tdr, rgs, rgr,
    mas, mar, mbs, mbr, xas, xar, xbs, xbr,
    axs, axr, ams, amr, ysm, yrm, zsm, zrm, f_s, f_r, d_s, d_r, lsem,
):
    nx, ny, nz = dims
    nr = 2 * nx
    tb, dc = tok.shape
    db, fb = gate_hbm.shape
    half = nz // 2

    row, col = lax.axis_index("row"), lax.axis_index("col")
    x, kap = lax.div(row, 2), lax.rem(row, 2)
    z, y = lax.div(col, ny), lax.rem(col, ny)
    mate = (x * 2 + 1 - kap, col)
    diag = row == z

    def xdev(d):
        return (lax.rem(x + d, nx) * 2 + kap, col)

    def ydev(d):
        return (row, z * ny + lax.rem(y + d, ny))

    def zdev(d):
        return (row, lax.rem(z + d, nz) * ny + y)

    def tdev(k):
        return (z, row * ny + k)

    def rows(t):
        return pl.ds(pl.multiple_of(t * tb, tb), tb)

    def lanes(k):
        return pl.ds(pl.multiple_of(k * dc, dc), dc)

    def rc(src, dst, ss, rs, dev):
        return pltpu.make_async_remote_copy(
            src_ref=src, dst_ref=dst, send_sem=ss, recv_sem=rs,
            device_id=dev, device_id_type=MESH,
        )

    cg = pltpu.make_async_copy(gate_hbm, gw.at[:, pl.ds(0, fb)], lsem.at[0])
    cu = pltpu.make_async_copy(up_hbm, gw.at[:, pl.ds(fb, fb)], lsem.at[1])
    cg.start()
    cu.start()

    bar = pltpu.get_barrier_semaphore()

    def greet(dev):
        pl.semaphore_signal(bar, inc=1, device_id=dev, device_id_type=MESH)

    greet(mate)
    for d in range(1, nx):
        greet(xdev(d))
    for d in range(1, ny):
        greet(ydev(d))
    for d in range(1, nz):
        greet(zdev(d))
    for k in range(ny):
        @pl.when(jnp.logical_not(jnp.logical_and(diag, y == k)))
        def _():
            greet(tdev(k))
    pl.semaphore_wait(bar, 1 + (nx - 1) + (ny - 1) + (nz - 1) + ny - jnp.where(diag, 1, 0))

    def is_self(k):
        return jnp.logical_and(diag, y == k)

    for k in range(ny):
        @pl.when(jnp.logical_not(is_self(k)))
        def _():
            dst = xg.at[rows(row), lanes(y)]
            rc(tok, dst, t1s.at[k, 0], t1r.at[y, 0], tdev(k)).start()
            dst = xg.at[rows(row), lanes(ny + y)]
            rc(cot, dst, t1s.at[k, 1], t1r.at[y, 1], tdev(k)).start()

        @pl.when(is_self(k))
        def _():
            xg[rows(z), lanes(y)] = tok[...]
            xg[rows(z), lanes(ny + y)] = cot[...]

    def frows(k):
        return pl.ds(pl.multiple_of(k * fb, fb), fb)

    for k in range(ny):
        @pl.when(jnp.logical_not(is_self(k)))
        def _():
            rc(down.at[frows(k)], dp.at[:, lanes(y)], tds.at[k], tdr.at[y], tdev(k)).start()

        @pl.when(is_self(k))
        def _():
            dp[:, lanes(y)] = down[frows(k)]

    for k in range(ny):
        @pl.when(jnp.logical_not(is_self(k)))
        def _():
            dst = xg.at[rows(z), lanes(k)]
            rc(dst, dst, t1s.at[k, 0], t1r.at[k, 0], tdev(k)).wait_recv()
            dst = xg.at[rows(z), lanes(ny + k)]
            rc(dst, dst, t1s.at[k, 1], t1r.at[k, 1], tdev(k)).wait_recv()

    cg.wait()
    cu.wait()

    def order(i):
        s = lax.div(i + 1, 2)
        return lax.rem(z + nz + s - 2 * s * lax.rem(i, 2), nz)

    def ring(t, way, s):
        dev = zdev(1) if way == 0 else zdev(nz - 1)
        return rc(xg.at[rows(t)], xg.at[rows(t)], rgs.at[way, s], rgr.at[way, s], dev)

    def ring_half(t, way):
        dev = zdev(1) if way == 0 else zdev(nz - 1)
        ref = xg.at[rows(t), pl.ds(way * db, db)]
        return rc(ref, ref, rgs.at[way, half], rgr.at[way, half], dev)

    def reduce_pair(t, acc, mr, xs, xr, ms_sem, mr_sem, xs_sem, xr_sem):
        xt = lax.div(t, 2)
        ref = mr.at[xt]
        rc(ref, ref, ms_sem.at[xt], mr_sem.at[xt], mate).wait_recv()

        @pl.when(xt == x)
        def _():
            acc[xt] = acc[xt] + mr[xt]

        @pl.when(xt != x)
        def _():
            d = lax.rem(xt - x + nx, nx)
            xs[d] = (acc[xt] + mr[xt]).astype(BF)
            rc(xs.at[d], xr.at[d], xs_sem.at[d], xr_sem.at[d], xdev(d)).start()

    set_a = (acc_a, mr_a, xs_a, xr_a, mas, mar, xas, xar)
    set_b = (acc_b, mr_b, xs_b, xr_b, mbs, mbr, xbs, xbr)

    def give(t, part, acc, ms, mr, s_sem, r_sem):
        xt = lax.div(t, 2)

        @pl.when(lax.rem(t, 2) == kap)
        def _():
            acc[xt] = part

        @pl.when(lax.rem(t, 2) != kap)
        def _():
            ms[xt] = part
            rc(ms.at[xt], mr.at[xt], s_sem.at[xt], r_sem.at[xt], mate).start()

    def step_a(i, carry):
        s = lax.div(i + 1, 2)
        odd = lax.rem(i, 2) == 1
        t = order(i)

        @pl.when(i == 0)
        def _():
            ring(t, 0, 1).start()
            ring(t, 1, 1).start()

        @pl.when(jnp.logical_and(odd, s < half))
        def _():
            ring(t, 0, s).wait_recv()

            @pl.when(s + 1 < half)
            def _():
                ring(t, 0, s + 1).start()

            @pl.when(s + 1 == half)
            def _():
                ring_half(t, 0).start()

        @pl.when(jnp.logical_and(jnp.logical_not(odd), s > 0))
        def _():
            ring(t, 1, s).wait_recv()

            @pl.when(s + 1 < half)
            def _():
                ring(t, 1, s + 1).start()

            @pl.when(s + 1 == half)
            def _():
                ring_half(t, 1).start()

        @pl.when(i == nz - 1)
        def _():
            ring_half(t, 0).wait_recv()
            ring_half(t, 1).wait_recv()

        part = nn(xg[rows(t), pl.ds(0, db)], gw[...])
        give(t, part, acc_a, ms_a, mr_a, mas, mar)

        before = order(jnp.maximum(i - 1, 0))

        @pl.when(jnp.logical_and(i > 0, lax.rem(before, 2) == kap))
        def _():
            reduce_pair(before, *set_a)

        return carry

    lax.fori_loop(0, nz, step_a, 0)

    for k in range(ny):
        @pl.when(jnp.logical_not(is_self(k)))
        def _():
            dst = dp.at[:, lanes(k)]
            rc(dst, dst, tds.at[k], tdr.at[k], tdev(k)).wait_recv()

    def step_b(i, carry):
        t = order(i)
        part = nt(xg[rows(t), pl.ds(db, db)], dp[...])
        give(t, part, acc_b, ms_b, mr_b, mbs, mbr)

        before = order(jnp.maximum(i - 1, 0))

        @pl.when(jnp.logical_and(i == 0, lax.rem(order(nz - 1), 2) == kap))
        def _():
            reduce_pair(order(nz - 1), *set_a)

        @pl.when(jnp.logical_and(i > 0, lax.rem(before, 2) == kap))
        def _():
            reduce_pair(before, *set_b)

        return carry

    lax.fori_loop(0, nz, step_b, 0)

    @pl.when(lax.rem(order(nz - 1), 2) == kap)
    def _():
        reduce_pair(order(nz - 1), *set_b)

    for d in range(1, nx):
        rc(xr_a.at[d], xr_a.at[d], xas.at[d], xar.at[d], xdev(d)).wait_recv()
        rc(xr_b.at[d], xr_b.at[d], xbs.at[d], xbr.at[d], xdev(d)).wait_recv()

    chunk = 16

    def point(i, carry):
        r0 = pl.multiple_of(i * chunk, chunk)
        here = pl.ds(r0, chunk)
        sa = acc_a[x, here, :]
        sb = acc_b[x, here, :]
        for d in range(1, nx):
            sa = sa + xr_a[d, here, :].astype(F32)
            sb = sb + xr_b[d, here, :].astype(F32)
        g, u = sa[:, :fb], sa[:, fb:]
        sig = jax.nn.sigmoid(g)
        sw = g * sig
        there = pl.ds(pl.multiple_of(row * tb + r0, chunk), chunk)
        hid[there, pl.ds(0, fb)] = (sw * u).astype(BF)
        hid[there, pl.ds(fb, fb)] = (sb * u * sig * (1.0 + g * (1.0 - sig))).astype(BF)
        hid[there, pl.ds(2 * fb, fb)] = (sb * sw).astype(BF)
        return carry

    lax.fori_loop(0, tb // chunk, point, 0)

    def hcopy(t, ss, rs, dev):
        return rc(hid.at[rows(t)], hid.at[rows(t)], ss, rs, dev)

    for d in range(1, nx):
        hcopy(row, axs.at[d], axr.at[d], xdev(d)).start()
    hcopy(row, ams.at[0], amr.at[0], mate).start()

    def dist(j):
        q = lax.div(j, 2)
        return jnp.where(lax.rem(q, 2) == 1, lax.div(q + 1, 2), lax.rem(nx - lax.div(q, 2), nx))

    def block(j):
        src = lax.rem(x - dist(j) + nx, nx)
        return src * 2 + jnp.where(lax.rem(j, 2) == 0, kap, 1 - kap)

    def ycopy(t, d):
        return rc(os.at[t, d - 1], yr.at[t, d - 1], ysm.at[t, d - 1], yrm.at[t, d - 1], ydev(d))

    def reduce_y(t):
        total = oown[t]
        for d in range(1, ny):
            ycopy(t, d).wait_recv()
            total = total + yr[t, d - 1].astype(F32)

        @pl.when(t == z)
        def _():
            zown[...] = total

        @pl.when(t != z)
        def _():
            d = lax.rem(t - z + nz, nz)
            zs[d] = total.astype(BF)
            rc(zs.at[d], zr.at[d], zsm.at[d], zrm.at[d], zdev(d)).start()

    def step_c(j, carry):
        t = block(j)
        d = dist(j)
        even = lax.rem(j, 2) == 0

        @pl.when(jnp.logical_and(even, d > 0))
        def _():
            hcopy(t, axs.at[d], axr.at[d], xdev(d)).wait_recv()
            hcopy(t, ams.at[d], amr.at[d], mate).start()

        @pl.when(jnp.logical_not(even))
        def _():
            hcopy(t, ams.at[d], amr.at[d], mate).wait_recv()

        o32[:, pl.ds(0, db)] = nn(hid[rows(t), pl.ds(0, fb)], dp[...])
        o32[:, pl.ds(db, db)] = nt(hid[rows(t), pl.ds(fb, 2 * fb)], gw[...])
        for e in range(1, ny):
            k = lax.rem(y + e, ny)
            os[t, e - 1, :, pl.ds(0, dc)] = o32[:, lanes(k)].astype(BF)
            os[t, e - 1, :, pl.ds(dc, dc)] = o32[:, lanes(ny + k)].astype(BF)
            ycopy(t, e).start()
        oown[t, :, pl.ds(0, dc)] = o32[:, lanes(y)]
        oown[t, :, pl.ds(dc, dc)] = o32[:, lanes(ny + y)]

        @pl.when(j > 0)
        def _():
            reduce_y(block(jnp.maximum(j - 1, 0)))

        return carry

    lax.fori_loop(0, nr, step_c, 0)

    for k in range(ny):
        dgs[k] = tn(hid[:, pl.ds(0, fb)], xg[:, pl.ds(db + k * dc, dc)]).astype(BF)

        @pl.when(jnp.logical_not(is_self(k)))
        def _():
            rc(dgs.at[k], dg_o.at[frows(y)], d_s.at[k], d_r.at[y], tdev(k)).start()

        @pl.when(is_self(k))
        def _():
            dg_o[frows(y)] = dgs[k]

    reduce_y(block(nr - 1))

    for k in range(ny):
        w = tn(xg[:, pl.ds(k * dc, dc)], hid[:, pl.ds(fb, 2 * fb)]).astype(BF)
        gg_o[pl.ds(k * dc, dc)] = w[:, :fb]
        ug_o[pl.ds(k * dc, dc)] = w[:, fb:]

    total = zown[...]
    for d in range(1, nz):
        rc(zr.at[d], zr.at[d], zsm.at[d], zrm.at[d], zdev(d)).wait_recv()
        total = total + zr[d].astype(F32)
    fs[...] = total.astype(BF)

    def fcopy(w):
        dst = out_o if w == 0 else tg_o
        return rc(fs.at[:, pl.ds(w * dc, dc)], dst, f_s.at[w], f_r.at[w], tdev(y))

    @pl.when(diag)
    def _():
        out_o[...] = fs[:, pl.ds(0, dc)]
        tg_o[...] = fs[:, pl.ds(dc, dc)]

    @pl.when(jnp.logical_not(diag))
    def _():
        fcopy(0).start()
        fcopy(1).start()
        fcopy(0).wait_recv()
        fcopy(1).wait_recv()

    for k in range(ny):
        @pl.when(jnp.logical_not(is_self(k)))
        def _():
            rc(dgs.at[k], dg_o.at[frows(k)], d_s.at[k], d_r.at[k], tdev(k)).wait_recv()

    @pl.when(jnp.logical_not(diag))
    def _():
        fcopy(0).wait_send()
        fcopy(1).wait_send()

    for k in range(ny):
        @pl.when(jnp.logical_not(is_self(k)))
        def _():
            rc(tok, tok, t1s.at[k, 0], t1r.at[k, 0], tdev(k)).wait_send()
            rc(cot, cot, t1s.at[k, 1], t1r.at[k, 1], tdev(k)).wait_send()
            rc(down.at[frows(k)], dp.at[:, lanes(y)], tds.at[k], tdr.at[k], tdev(k)).wait_send()
            rc(dgs.at[k], dgs.at[k], d_s.at[k], d_r.at[k], tdev(k)).wait_send()

    for way in range(2):
        for s in range(1, half):
            ring(z, way, s).wait_send()
        ring_half(z, way).wait_send()

    for q in range(nx):
        rc(ms_a.at[q], mr_a.at[q], mas.at[q], mar.at[q], mate).wait_send()
        rc(ms_b.at[q], mr_b.at[q], mbs.at[q], mbr.at[q], mate).wait_send()
        hcopy(row, ams.at[q], amr.at[q], mate).wait_send()
    for d in range(1, nx):
        rc(xs_a.at[d], xr_a.at[d], xas.at[d], xar.at[d], xdev(d)).wait_send()
        rc(xs_b.at[d], xr_b.at[d], xbs.at[d], xbr.at[d], xdev(d)).wait_send()
        hcopy(row, axs.at[d], axr.at[d], xdev(d)).wait_send()
    for d in range(1, nz):
        rc(zs.at[d], zr.at[d], zsm.at[d], zrm.at[d], zdev(d)).wait_send()

    def ydone(t, carry):
        for d in range(1, ny):
            ycopy(t, d).wait_send()
        return carry

    lax.fori_loop(0, nr, ydone, 0)


def local(dims, tokens, gate_weight, up_weight, down_weight, out_grad):
    nx, ny, nz = dims
    nr = 2 * nx
    tb, dc = tokens.shape
    db, fb = gate_weight.shape
    t = nr * tb
    vm = pl.BlockSpec(memory_space=pltpu.VMEM)
    hbm = pl.BlockSpec(memory_space=pl.ANY)
    dma = pltpu.SemaphoreType.DMA
    half = nz // 2

    def pair(width):
        return [
            pltpu.VMEM((nx, tb, width), F32),
            pltpu.VMEM((nx, tb, width), F32),
            pltpu.VMEM((nx, tb, width), F32),
            pltpu.VMEM((nx, tb, width), BF),
            pltpu.VMEM((nx, tb, width), BF),
        ]

    scratch = [
        pltpu.VMEM((t, 2 * db), BF),
        pltpu.VMEM((db, 2 * fb), BF),
        pltpu.VMEM((fb, db), BF),
        pltpu.VMEM((t, 3 * fb), BF),
        *pair(2 * fb),
        *pair(fb),
        pltpu.VMEM((tb, 2 * db), F32),
        pltpu.VMEM((nr, ny - 1, tb, 2 * dc), BF),
        pltpu.VMEM((nr, tb, 2 * dc), F32),
        pltpu.VMEM((nr, ny - 1, tb, 2 * dc), BF),
        pltpu.VMEM((nz, tb, 2 * dc), BF),
        pltpu.VMEM((nz, tb, 2 * dc), BF),
        pltpu.VMEM((tb, 2 * dc), F32),
        pltpu.VMEM((tb, 2 * dc), BF),
        pltpu.VMEM((ny, fb, dc), BF),
        dma((ny, 2)), dma((ny, 2)), dma((ny,)), dma((ny,)),
        dma((2, half + 1)), dma((2, half + 1)),
        *[dma((nx,))] * 8,
        *[dma((nx,))] * 4,
        dma((nr, ny - 1)), dma((nr, ny - 1)), dma((nz,)), dma((nz,)),
        dma((2,)), dma((2,)), dma((ny,)), dma((ny,)), dma((2,)),
    ]
    shape = jax.ShapeDtypeStruct
    return pl.pallas_call(
        functools.partial(kernel, dims),
        out_shape=(
            shape((tb, dc), BF),
            shape((tb, dc), BF),
            shape((db, fb), BF),
            shape((db, fb), BF),
            shape((ny * fb, dc), BF),
        ),
        in_specs=[vm, vm, hbm, hbm, vm],
        out_specs=(vm,) * 5,
        scratch_shapes=scratch,
        compiler_params=pltpu.CompilerParams(
            collective_id=0, has_side_effects=True, vmem_limit_bytes=50 * 2**20
        ),
        name="swiglu",
    )(tokens, out_grad, gate_weight, up_weight, down_weight)


def solution(mesh):
    nr, nc = mesh.shape["row"], mesh.shape["col"]
    dims = (nr // 2, nc // nr, nr)
    spec = P("row", "col")
    return jax.shard_map(
        functools.partial(local, dims),
        mesh=mesh,
        in_specs=(spec,) * 5,
        out_specs=(spec,) * 5,
        check_vma=False,
    )
```

time: 823 us -> 191 us (0.23)
  the two profiles are of different devices: /device:TPU:4 before, /device:TPU:2 now
where the time goes in v1:
time: 191 us; the launch traced here: 190 us
  Pallas kernels  181 us (95%)
  local copies, waits for them, and re-layouts  8.24 us (4%)
    pallas_call x1, Pallas kernels, local(): pl.pallas_call(functools.partial(kernel, dims), out_shape=(shape((tb, dc)...  181 us
    unnamed x15, local copies, waits for them, and re-layouts  8.24 us

profile of v1, /device:TPU:2, one launch (start us, length us, event | category | flops | bytes accessed | tf_op | source)
XLA Modules:
  0.0 190.3 jit_solution(12528515420493739181)
XLA Ops:
  0.6 0.0 copy-start
  0.6 1.0 copy-done
  1.7 0.0 copy-start.1
  1.7 1.0 copy-done.1
  2.7 0.0 copy-start.2
  2.7 1.0 copy-done.2
  3.8 0.0 copy-start.3
  3.8 0.8 copy-done.3
  4.5 0.0 copy-start.4
  4.5 0.8 copy-done.4
  5.3 181.4 %swiglu.1 = (bf16[128,128]{1,0:T(8,128)(2,1)S(1)}, bf16[128,128]{1,0:T(8,128)(2,1)S(1)}, bf16[512,512]{1,0:T(8,128)(2,1)S(1)}, bf16[512,512]{1,0:T(8,128)(2,1)S(1)}, bf16[2048,128]{1,0:T(8,128)(2,1)S(1)}) custom-call(bf16[128,128]{1,0:T(8,128)(2,1)S(1)} %copy-done.3, bf16[128,128]{1,0:T(8,128)(2,1)S(1)} %copy-done.4, bf16[512,512]{1,0:T(8,128)(2,1)S(1)} %copy-done, ...), custom_call_target="tpu_custom_call" | custom-call | tf_op jit(solution)/shard_map/swiglu/pallas_call | solution.py:478
  186.7 0.6 copy.15
  187.3 0.6 copy.16
  187.9 0.8 copy.17
  188.7 0.8 copy.18
  189.5 0.8 copy.19
Async XLA Ops:
  0.6 1.0 copy-start
  1.7 1.0 copy-start.1
  2.7 1.0 copy-start.2
  3.8 0.8 copy-start.3
  4.5 0.8 copy-start.4

commit v2 on v1

v2 whole, which is shorter than its diff:
```python
import functools

import jax
import jax.numpy as jnp
from jax import lax
from jax.experimental import pallas as pl
from jax.experimental.pallas import tpu as pltpu
from jax.sharding import PartitionSpec as P

MESH = pl.DeviceIdType.MESH
BF = jnp.bfloat16
F32 = jnp.float32


def nn(a, b):
    return lax.dot_general(a, b, (((1,), (0,)), ((), ())), preferred_element_type=F32)


def nt(a, b):
    return lax.dot_general(a, b, (((1,), (1,)), ((), ())), preferred_element_type=F32)


def tn(a, b):
    return lax.dot_general(a, b, (((0,), (0,)), ((), ())), preferred_element_type=F32)


def kernel(
    dims,
    tok, cot, gate_hbm, up_hbm, down,
    out_o, tg_o, gg_o, ug_o, dg_o,
    xg, gw, dp, hh, hg, mid, mid2,
    acc_a, ms_a, mr_a, xs_a, xr_a,
    acc_b, ms_b, mr_b, xs_b, xr_b,
    o32, os_o, own_o, yr_o, os_t, own_t, yr_t,
    zs, zr, zown, fs, dgs,
    t1s, t1r, tys, tyr, trs, trr, crs, crr, cys, cyr,
    d1s, d1r, d2s, d2r, e1s, e1r, e2s, e2r,
    mas, mar, mbs, mbr, xas, xar, xbs, xbr,
    hxs, hxr, hms, hmr, gxs, gxr, gms, gmr,
    yos, yor, yts, ytr, zsm, zrm, f_s, f_r, lsem,
):
    nx, ny, nz = dims
    nr = 2 * nx
    tb, dc = tok.shape
    db, fb = gate_hbm.shape
    half = nz // 2

    row, col = lax.axis_index("row"), lax.axis_index("col")
    x, kap = lax.div(row, 2), lax.rem(row, 2)
    z, y = lax.div(col, ny), lax.rem(col, ny)
    mate = (x * 2 + 1 - kap, col)
    diag = row == z
    twin = (z, row * ny + y)

    def xdev(d):
        return (lax.rem(x + d, nx) * 2 + kap, col)

    def ydev(d):
        return (row, z * ny + lax.rem(y + d, ny))

    def zdev(d):
        return (row, lax.rem(z + d, nz) * ny + y)

    def leg1_to(k):
        return (lax.rem(x + y - k + 1 + nx, nx) * 2 + kap, z * ny + k)

    def leg1_from(s):
        return (lax.rem(x + y - s - 1 + 2 * nx, nx) * 2 + kap, z * ny + s)

    def leg2_to(s):
        return (z, (lax.rem(x + y - s - 1 + 2 * nx, nx) * 2 + kap) * ny + y)

    def leg2_from(s):
        return (lax.rem(lax.div(z, 2) + s - y + 1 + nx, nx) * 2 + lax.rem(z, 2), row * ny + y)

    def leg2_home(s):
        return jnp.logical_and(diag, lax.rem(x + y - s - 1 + 2 * nx, nx) == x)

    def leg2_kept(s):
        return jnp.logical_and(diag, lax.rem(x + s - y + 1 + nx, nx) == x)

    def rows(t):
        return pl.ds(pl.multiple_of(t * tb, tb), tb)

    def lanes(k):
        return pl.ds(pl.multiple_of(k * dc, dc), dc)

    def frows(k):
        return pl.ds(pl.multiple_of(k * fb, fb), fb)

    def rc(src, dst, ss, rs, dev):
        return pltpu.make_async_remote_copy(
            src_ref=src, dst_ref=dst, send_sem=ss, recv_sem=rs,
            device_id=dev, device_id_type=MESH,
        )

    def no(cond):
        return jnp.logical_not(cond)

    cg = pltpu.make_async_copy(gate_hbm, gw.at[:, pl.ds(0, fb)], lsem.at[0])
    cu = pltpu.make_async_copy(up_hbm, gw.at[:, pl.ds(fb, fb)], lsem.at[1])
    cg.start()
    cu.start()

    bar = pltpu.get_barrier_semaphore()

    def greet(dev):
        pl.semaphore_signal(bar, inc=1, device_id=dev, device_id_type=MESH)

    greet(mate)
    for d in range(1, nx):
        greet(xdev(d))
    for d in range(1, ny):
        greet(ydev(d))
    for d in range(1, nz):
        greet(zdev(d))

    @pl.when(no(diag))
    def _():
        greet(twin)

    count = 1 + (nx - 1) + (ny - 1) + (nz - 1) + 2 * ny + jnp.where(diag, 0, 1)
    for s in range(ny):
        greet(leg1_to(s))
        greet(leg1_from(s))

        @pl.when(no(leg2_home(s)))
        def _():
            greet(leg2_to(s))

        @pl.when(no(leg2_kept(s)))
        def _():
            greet(leg2_from(s))

        count = count + jnp.where(leg2_home(s), 0, 1) + jnp.where(leg2_kept(s), 0, 1)
    pl.semaphore_wait(bar, count)

    def mine(w):
        return lanes(w * ny + y)

    @pl.when(no(diag))
    def _():
        rc(tok, xg.at[rows(row), mine(0)], t1s.at[0], t1r.at[0], twin).start()
        rc(cot, xg.at[rows(row), mine(1)], t1s.at[1], t1r.at[1], twin).start()

    @pl.when(diag)
    def _():
        xg[rows(z), mine(0)] = tok[...]
        xg[rows(z), mine(1)] = cot[...]

    for k in range(ny):
        rc(down.at[frows(k)], mid.at[y], d1s.at[k], d1r.at[y], leg1_to(k)).start()

    def ty(d):
        ref = xg.at[rows(z), mine(0)]
        return rc(ref, ref, tys.at[d], tyr.at[d], ydev(d))

    def tring(t, way, s):
        ref = xg.at[rows(t), pl.ds(0, db)]
        return rc(ref, ref, trs.at[way, s], trr.at[way, s], zdev(1 if way == 0 else nz - 1))

    def tring_half(t, way):
        ref = xg.at[rows(t), pl.ds(way * (db // 2), db // 2)]
        return rc(ref, ref, trs.at[way, half], trr.at[way, half], zdev(1 if way == 0 else nz - 1))

    def cring(t, way, s):
        ref = xg.at[rows(t), mine(1)]
        return rc(ref, ref, crs.at[way, s], crr.at[way, s], zdev(1 if way == 0 else nz - 1))

    def cring_half(t, way):
        ht = tb // 2
        ref = xg.at[pl.ds(pl.multiple_of(t * tb + way * ht, ht), ht), mine(1)]
        return rc(ref, ref, crs.at[way, half], crr.at[way, half], zdev(1 if way == 0 else nz - 1))

    def cy(t, d):
        ref = xg.at[rows(t), mine(1)]
        return rc(ref, ref, cys.at[t, d - 1], cyr.at[t, d - 1], ydev(d))

    @pl.when(no(diag))
    def _():
        ref = xg.at[rows(z), mine(0)]
        rc(ref, ref, t1s.at[0], t1r.at[0], twin).wait_recv()

    for d in range(1, ny):
        ty(d).start()

    @pl.when(no(diag))
    def _():
        ref = xg.at[rows(z), mine(1)]
        rc(ref, ref, t1s.at[1], t1r.at[1], twin).wait_recv()

    cring(z, 0, 1).start()
    cring(z, 1, 1).start()
    for d in range(1, ny):
        cy(z, d).start()

    cg.wait()
    cu.wait()

    for d in range(1, ny):
        ty(d).wait_recv()

    def order(i):
        s = lax.div(i + 1, 2)
        return lax.rem(z + nz + s - 2 * s * lax.rem(i, 2), nz)

    def pass_on(i, full, part):
        s = lax.div(i + 1, 2)
        odd = lax.rem(i, 2) == 1
        t = order(i)
        for way in range(2):
            side = odd if way == 0 else jnp.logical_and(no(odd), s > 0)

            @pl.when(jnp.logical_and(side, s < half))
            def _():
                full(t, way, s).wait_recv()

                @pl.when(s + 1 < half)
                def _():
                    full(t, way, s + 1).start()

                @pl.when(s + 1 == half)
                def _():
                    part(t, way).start()

        @pl.when(i == nz - 1)
        def _():
            part(t, 0).wait_recv()
            part(t, 1).wait_recv()

    def reduce_pair(t, acc, mr, xs, xr, ms_sem, mr_sem, xs_sem, xr_sem):
        xt = lax.div(t, 2)
        ref = mr.at[xt]
        rc(ref, ref, ms_sem.at[xt], mr_sem.at[xt], mate).wait_recv()

        @pl.when(xt == x)
        def _():
            acc[xt] = acc[xt] + mr[xt]

        @pl.when(xt != x)
        def _():
            d = lax.rem(xt - x + nx, nx)
            xs[d] = (acc[xt] + mr[xt]).astype(BF)
            rc(xs.at[d], xr.at[d], xs_sem.at[d], xr_sem.at[d], xdev(d)).start()

    set_a = (acc_a, mr_a, xs_a, xr_a, mas, mar, xas, xar)
    set_b = (acc_b, mr_b, xs_b, xr_b, mbs, mbr, xbs, xbr)

    def give(t, part, acc, ms, mr, s_sem, r_sem):
        xt = lax.div(t, 2)

        @pl.when(lax.rem(t, 2) == kap)
        def _():
            acc[xt] = part

        @pl.when(lax.rem(t, 2) != kap)
        def _():
            ms[xt] = part
            rc(ms.at[xt], mr.at[xt], s_sem.at[xt], r_sem.at[xt], mate).start()

    def leg2(src, dst_of, s1, r1, s2, r2, s):
        ref = src.at[s]
        rc(ref, ref, s1.at[s], r1.at[s], leg1_from(s)).wait_recv()

        @pl.when(no(leg2_home(s)))
        def _():
            rc(ref, dst_of(s), s2.at[s], r2.at[s], leg2_to(s)).start()

        @pl.when(leg2_home(s))
        def _():
            pltpu.make_async_copy(ref, dst_of(s), lsem.at[2]).start()
            pltpu.make_async_copy(ref, dst_of(s), lsem.at[2]).wait()

    def dp_at(s):
        return dp.at[:, lanes(s)]

    def dg_at(s):
        return dg_o.at[frows(s)]

    tring(z, 0, 1).start()
    tring(z, 1, 1).start()

    def step_a(i, carry):
        t = order(i)
        pass_on(i, tring, tring_half)
        part = nn(xg[rows(t), pl.ds(0, db)], gw[...])
        give(t, part, acc_a, ms_a, mr_a, mas, mar)

        before = order(jnp.maximum(i - 1, 0))

        @pl.when(jnp.logical_and(i > 0, lax.rem(before, 2) == kap))
        def _():
            reduce_pair(before, *set_a)

        pass_on(i, cring, cring_half)

        @pl.when(i > 0)
        def _():
            for d in range(1, ny):
                cy(t, d).start()

        @pl.when(i == 1)
        def _():
            for s in range(ny):
                leg2(mid, dp_at, d1s, d1r, d2s, d2r, s)

        return carry

    lax.fori_loop(0, nz, step_a, 0)

    @pl.when(lax.rem(order(nz - 1), 2) == kap)
    def _():
        reduce_pair(order(nz - 1), *set_a)

    for s in range(ny):
        @pl.when(no(leg2_kept(s)))
        def _():
            rc(dp_at(s), dp_at(s), d2s.at[s], d2r.at[s], leg2_from(s)).wait_recv()

    def step_b(i, carry):
        t = order(i)
        for d in range(1, ny):
            ref = xg.at[rows(t), lanes(ny + lax.rem(y - d + ny, ny))]
            rc(ref, ref, cys.at[t, d - 1], cyr.at[t, d - 1], ydev(d)).wait_recv()
        part = nt(xg[rows(t), pl.ds(db, db)], dp[...])
        give(t, part, acc_b, ms_b, mr_b, mbs, mbr)

        before = order(jnp.maximum(i - 1, 0))

        @pl.when(jnp.logical_and(i > 0, lax.rem(before, 2) == kap))
        def _():
            reduce_pair(before, *set_b)

        return carry

    lax.fori_loop(0, nz, step_b, 0)

    @pl.when(lax.rem(order(nz - 1), 2) == kap)
    def _():
        reduce_pair(order(nz - 1), *set_b)

    chunk = 16

    def spot(i):
        r0 = pl.multiple_of(i * chunk, chunk)
        return pl.ds(r0, chunk), pl.ds(pl.multiple_of(row * tb + r0, chunk), chunk)

    for d in range(1, nx):
        rc(xr_a.at[d], xr_a.at[d], xas.at[d], xar.at[d], xdev(d)).wait_recv()

    def point_h(i, carry):
        here, there = spot(i)
        sa = acc_a[x, here, :]
        for d in range(1, nx):
            sa = sa + xr_a[d, here, :].astype(F32)
        acc_a[x, here, :] = sa
        g, u = sa[:, :fb], sa[:, fb:]
        hh[there, :] = (g * jax.nn.sigmoid(g) * u).astype(BF)
        return carry

    lax.fori_loop(0, tb // chunk, point_h, 0)

    def hcopy(buf, t, ss, rs, dev):
        return rc(buf.at[rows(t)], buf.at[rows(t)], ss, rs, dev)

    def share(buf, xs_sem, xr_sem, ms_sem, mr_sem):
        hcopy(buf, row, ms_sem.at[0], mr_sem.at[0], mate).start()
        for d in range(1, nx):
            hcopy(buf, row, xs_sem.at[d], xr_sem.at[d], xdev(d)).start()

    share(hh, hxs, hxr, hms, hmr)

    for d in range(1, nx):
        rc(xr_b.at[d], xr_b.at[d], xbs.at[d], xbr.at[d], xdev(d)).wait_recv()

    def point_g(i, carry):
        here, there = spot(i)
        sa = acc_a[x, here, :]
        sb = acc_b[x, here, :]
        for d in range(1, nx):
            sb = sb + xr_b[d, here, :].astype(F32)
        g, u = sa[:, :fb], sa[:, fb:]
        sig = jax.nn.sigmoid(g)
        hg[there, pl.ds(0, fb)] = (sb * u * sig * (1.0 + g * (1.0 - sig))).astype(BF)
        hg[there, pl.ds(fb, fb)] = (sb * (g * sig)).astype(BF)
        return carry

    lax.fori_loop(0, tb // chunk, point_g, 0)
    share(hg, gxs, gxr, gms, gmr)

    def dist(j):
        q = lax.div(j, 2)
        return jnp.where(lax.rem(q, 2) == 1, lax.div(q + 1, 2), lax.rem(nx - lax.div(q, 2), nx))

    def block(j):
        src = lax.rem(x - dist(j) + nx, nx)
        return src * 2 + jnp.where(lax.rem(j, 2) == 0, kap, 1 - kap)

    def arrive(buf, j, xs_sem, xr_sem, ms_sem, mr_sem):
        t, d = block(j), dist(j)
        even = lax.rem(j, 2) == 0

        @pl.when(jnp.logical_and(even, d > 0))
        def _():
            hcopy(buf, t, xs_sem.at[d], xr_sem.at[d], xdev(d)).wait_recv()
            hcopy(buf, t, ms_sem.at[d], mr_sem.at[d], mate).start()

        @pl.when(no(even))
        def _():
            hcopy(buf, t, ms_sem.at[d], mr_sem.at[d], mate).wait_recv()

    def ycopy(w, t, d):
        os, yr, ss, rs = ((os_o, yr_o, yos, yor), (os_t, yr_t, yts, ytr))[w]
        return rc(os.at[t, d - 1], yr.at[t, d - 1], ss.at[t, d - 1], rs.at[t, d - 1], ydev(d))

    def spread(w, t, part):
        os, own = ((os_o, own_o), (os_t, own_t))[w]
        o32[...] = part
        for e in range(1, ny):
            os[t, e - 1] = o32[:, lanes(lax.rem(y + e, ny))].astype(BF)
            ycopy(w, t, e).start()
        own[t] = o32[:, lanes(y)]

    def zcopy(w, d):
        return rc(zs.at[w, d], zr.at[w, d], zsm.at[w, d], zrm.at[w, d], zdev(d))

    def reduce_y(w, t):
        own, yr = ((own_o, yr_o), (own_t, yr_t))[w]
        total = own[t]
        for d in range(1, ny):
            ycopy(w, t, d).wait_recv()
            total = total + yr[t, d - 1].astype(F32)

        @pl.when(t == z)
        def _():
            zown[w] = total

        @pl.when(t != z)
        def _():
            d = lax.rem(t - z + nz, nz)
            zs[w, d] = total.astype(BF)
            zcopy(w, d).start()

    def step_c(j, carry):
        arrive(hh, j, hxs, hxr, hms, hmr)
        t = block(j)
        spread(0, t, nn(hh[rows(t), :], dp[...]))
        return carry

    lax.fori_loop(0, nr, step_c, 0)

    for k in range(ny):
        dgs[k] = tn(hh[...], xg[:, pl.ds(db + k * dc, dc)]).astype(BF)
        rc(dgs.at[k], mid2.at[y], e1s.at[k], e1r.at[y], leg1_to(k)).start()

    lag = 2

    def step_d(j, carry):
        arrive(hg, j, gxs, gxr, gms, gmr)
        t = block(j)
        spread(1, t, nt(hg[rows(t), :], gw[...]))
        reduce_y(0, t)

        @pl.when(j >= lag)
        def _():
            reduce_y(1, block(jnp.maximum(j - lag, 0)))

        @pl.when(j == nr // 2)
        def _():
            for s in range(ny):
                leg2(mid2, dg_at, e1s, e1r, e2s, e2r, s)

        return carry

    lax.fori_loop(0, nr, step_d, 0)

    for k in range(ny):
        w = tn(xg[:, pl.ds(k * dc, dc)], hg[...]).astype(BF)
        gg_o[pl.ds(k * dc, dc)] = w[:, :fb]
        ug_o[pl.ds(k * dc, dc)] = w[:, fb:]

    for j in range(nr - lag, nr):
        reduce_y(1, block(j))

    def fcopy(w):
        return rc(fs.at[w], (out_o, tg_o)[w], f_s.at[w], f_r.at[w], twin)

    for w in range(2):
        total = zown[w]
        for d in range(1, nz):
            zcopy(w, d).wait_recv()
            total = total + zr[w, d].astype(F32)
        fs[w] = total.astype(BF)

        @pl.when(diag)
        def _():
            (out_o, tg_o)[w][...] = fs[w]

        @pl.when(no(diag))
        def _():
            fcopy(w).start()

    @pl.when(no(diag))
    def _():
        for w in range(2):
            fcopy(w).wait_recv()

    for s in range(ny):
        @pl.when(no(leg2_kept(s)))
        def _():
            rc(dg_at(s), dg_at(s), e2s.at[s], e2r.at[s], leg2_from(s)).wait_recv()

    @pl.when(no(diag))
    def _():
        for w in range(2):
            fcopy(w).wait_send()
        rc(tok, tok, t1s.at[0], t1r.at[0], twin).wait_send()
        rc(cot, cot, t1s.at[1], t1r.at[1], twin).wait_send()

    for k in range(ny):
        rc(dgs.at[k], mid.at[k], d1s.at[k], d1r.at[k], leg1_to(k)).wait_send()
        rc(dgs.at[k], mid.at[k], e1s.at[k], e1r.at[k], leg1_to(k)).wait_send()

        @pl.when(no(leg2_home(k)))
        def _():
            rc(mid.at[k], dp_at(k), d2s.at[k], d2r.at[k], leg2_to(k)).wait_send()
            rc(mid2.at[k], dg_at(k), e2s.at[k], e2r.at[k], leg2_to(k)).wait_send()

    for d in range(1, ny):
        ty(d).wait_send()
    for way in range(2):
        for s in range(1, half):
            tring(z, way, s).wait_send()
            cring(z, way, s).wait_send()
        tring_half(z, way).wait_send()
        cring_half(z, way).wait_send()

    for q in range(nx):
        rc(ms_a.at[q], mr_a.at[q], mas.at[q], mar.at[q], mate).wait_send()
        rc(ms_b.at[q], mr_b.at[q], mbs.at[q], mbr.at[q], mate).wait_send()
        hcopy(hh, row, hms.at[q], hmr.at[q], mate).wait_send()
        hcopy(hg, row, gms.at[q], gmr.at[q], mate).wait_send()
    for d in range(1, nx):
        rc(xs_a.at[d], xr_a.at[d], xas.at[d], xar.at[d], xdev(d)).wait_send()
        rc(xs_b.at[d], xr_b.at[d], xbs.at[d], xbr.at[d], xdev(d)).wait_send()
        hcopy(hh, row, hxs.at[d], hxr.at[d], xdev(d)).wait_send()
        hcopy(hg, row, gxs.at[d], gxr.at[d], xdev(d)).wait_send()
    for d in range(1, nz):
        zcopy(0, d).wait_send()
        zcopy(1, d).wait_send()

    def ydone(t, carry):
        for d in range(1, ny):
            cy(t, d).wait_send()
            ycopy(0, t, d).wait_send()
            ycopy(1, t, d).wait_send()
        return carry

    lax.fori_loop(0, nr, ydone, 0)


def local(dims, tokens, gate_weight, up_weight, down_weight, out_grad):
    nx, ny, nz = dims
    nr = 2 * nx
    tb, dc = tokens.shape
    db, fb = gate_weight.shape
    t = nr * tb
    vm = pl.BlockSpec(memory_space=pltpu.VMEM)
    hbm = pl.BlockSpec(memory_space=pl.ANY)
    dma = pltpu.SemaphoreType.DMA
    half = nz // 2

    def sums(width):
        return [
            pltpu.VMEM((nx, tb, width), F32),
            pltpu.VMEM((nx, tb, width), F32),
            pltpu.VMEM((nx, tb, width), F32),
            pltpu.VMEM((nx, tb, width), BF),
            pltpu.VMEM((nx, tb, width), BF),
        ]

    def shares():
        return [
            pltpu.VMEM((nr, ny - 1, tb, dc), BF),
            pltpu.VMEM((nr, tb, dc), F32),
            pltpu.VMEM((nr, ny - 1, tb, dc), BF),
        ]

    scratch = [
        pltpu.VMEM((t, 2 * db), BF),
        pltpu.VMEM((db, 2 * fb), BF),
        pltpu.VMEM((fb, db), BF),
        pltpu.VMEM((t, fb), BF),
        pltpu.VMEM((t, 2 * fb), BF),
        pltpu.VMEM((ny, fb, dc), BF),
        pltpu.VMEM((ny, fb, dc), BF),
        *sums(2 * fb),
        *sums(fb),
        pltpu.VMEM((tb, db), F32),
        *shares(),
        *shares(),
        pltpu.VMEM((2, nz, tb, dc), BF),
        pltpu.VMEM((2, nz, tb, dc), BF),
        pltpu.VMEM((2, tb, dc), F32),
        pltpu.VMEM((2, tb, dc), BF),
        pltpu.VMEM((ny, fb, dc), BF),
        dma((2,)), dma((2,)), dma((ny,)), dma((ny,)),
        *[dma((2, half + 1))] * 4,
        dma((nr, ny - 1)), dma((nr, ny - 1)),
        *[dma((ny,))] * 8,
        *[dma((nx,))] * 16,
        *[dma((nr, ny - 1))] * 4,
        dma((2, nz)), dma((2, nz)), dma((2,)), dma((2,)), dma((3,)),
    ]
    shape = jax.ShapeDtypeStruct
    return pl.pallas_call(
        functools.partial(kernel, dims),
        out_shape=(
            shape((tb, dc), BF),
            shape((tb, dc), BF),
            shape((db, fb), BF),
            shape((db, fb), BF),
            shape((ny * fb, dc), BF),
        ),
        in_specs=[vm, vm, hbm, hbm, vm],
        out_specs=(vm,) * 5,
        scratch_shapes=scratch,
        compiler_params=pltpu.CompilerParams(
            collective_id=0, has_side_effects=True, vmem_limit_bytes=50 * 2**20
        ),
        name="swiglu",
    )(tokens, out_grad, gate_weight, up_weight, down_weight)


def solution(mesh):
    nr, nc = mesh.shape["row"], mesh.shape["col"]
    dims = (nr // 2, nc // nr, nr)
    spec = P("row", "col")
    return jax.shard_map(
        functools.partial(local, dims),
        mesh=mesh,
        in_specs=(spec,) * 5,
        out_specs=(spec,) * 5,
        check_vma=False,
    )
```

time: 191 us -> 138 us (0.72)
  the two profiles are of different devices: /device:TPU:2 before, /device:TPU:4 now
where the time goes in v2:
time: 138 us; the launch traced here: 137 us
  Pallas kernels  128 us (93%)
  local copies, waits for them, and re-layouts  8.24 us (6%)
    pallas_call x1, Pallas kernels, local(): pl.pallas_call(functools.partial(kernel, dims), out_shape=(shape((tb, dc)...  128 us
    unnamed x15, local copies, waits for them, and re-layouts  8.24 us

profile of v2, /device:TPU:4, one launch (start us, length us, event | category | flops | bytes accessed | tf_op | source)
XLA Modules:
  0.0 136.6 jit_solution(13348207744367395097)
XLA Ops:
  0.6 0.0 copy-start
  0.6 1.0 copy-done
  1.7 0.0 copy-start.1
  1.7 1.0 copy-done.1
  2.7 0.0 copy-start.2
  2.7 1.0 copy-done.2
  3.8 0.0 copy-start.3
  3.8 0.8 copy-done.3
  4.5 0.0 copy-start.4
  4.5 0.8 copy-done.4
  5.3 127.7 %swiglu.1 = (bf16[128,128]{1,0:T(8,128)(2,1)S(1)}, bf16[128,128]{1,0:T(8,128)(2,1)S(1)}, bf16[512,512]{1,0:T(8,128)(2,1)S(1)}, bf16[512,512]{1,0:T(8,128)(2,1)S(1)}, bf16[2048,128]{1,0:T(8,128)(2,1)S(1)}) custom-call(bf16[128,128]{1,0:T(8,128)(2,1)S(1)} %copy-done.3, bf16[128,128]{1,0:T(8,128)(2,1)S(1)} %copy-done.4, bf16[512,512]{1,0:T(8,128)(2,1)S(1)} %copy-done, ...), custom_call_target="tpu_custom_call" | custom-call | tf_op jit(solution)/shard_map/swiglu/pallas_call | solution.py:616
  133.0 0.6 copy.15
  133.6 0.6 copy.16
  134.2 0.8 copy.17
  135.0 0.8 copy.18
  135.8 0.8 copy.19
Async XLA Ops:
  0.6 1.0 copy-start
  1.7 1.0 copy-start.1
  2.7 1.0 copy-start.2
  3.8 0.8 copy-start.3
  4.5 0.8 copy-start.4

commit v3 on v2

v3 whole, which is shorter than its diff:
```python
import functools

import jax
import jax.numpy as jnp
from jax import lax
from jax.experimental import pallas as pl
from jax.experimental.pallas import tpu as pltpu
from jax.sharding import PartitionSpec as P

MESH = pl.DeviceIdType.MESH
BF = jnp.bfloat16
F32 = jnp.float32


def nn(a, b):
    return lax.dot_general(a, b, (((1,), (0,)), ((), ())), preferred_element_type=F32)


def nt(a, b):
    return lax.dot_general(a, b, (((1,), (1,)), ((), ())), preferred_element_type=F32)


def tn(a, b):
    return lax.dot_general(a, b, (((0,), (0,)), ((), ())), preferred_element_type=F32)


def kernel(
    dims,
    tok_hbm, cot_hbm, gate_hbm, up_hbm, down_hbm,
    out_o, tg_o, gg_o, ug_o, dg_o,
    tok, cot, down, xg, gw, dp, hh, hg, mid, mid2,
    acc_a, ms_a, mr_a, xs_a, xr_a,
    acc_b, ms_b, mr_b, xs_b, xr_b,
    o32, os_o, own_o, yr_o, os_t, own_t, yr_t,
    zs, zr, zown, fs, dgs,
    tos, tor, cos, cor, tys, tyr, cys, cyr,
    d1s, d1r, d2s, d2r, e1s, e1r, e2s, e2r,
    mas, mar, mbs, mbr, xas, xar, xbs, xbr,
    hxs, hxr, hms, hmr, gxs, gxr, gms, gmr,
    yos, yor, yts, ytr, zsm, zrm, f_s, f_r, lsem,
):
    nx, ny, nz = dims
    nr = 2 * nx
    tb, dc = tok.shape
    db, fb = gate_hbm.shape

    row, col = lax.axis_index("row"), lax.axis_index("col")
    x, kap = lax.div(row, 2), lax.rem(row, 2)
    z, y = lax.div(col, ny), lax.rem(col, ny)
    mate = (x * 2 + 1 - kap, col)
    diag = row == z
    twin = (z, row * ny + y)

    near = sorted({1, nx - 1})
    opposite = nx // 2 if nx > 2 else 0

    def xdev(d):
        return (lax.rem(x + d, nx) * 2 + kap, col)

    def ydev(d):
        return (row, z * ny + lax.rem(y + d, ny))

    def zdev(d):
        return (row, lax.rem(z + d, nz) * ny + y)

    def panel_to(d):
        return (z, lax.rem(z + d, nz) * ny + y)

    def panel_from(r):
        return (r, row * ny + y)

    def leg1_to(k):
        return (lax.rem(x + y - k + 1 + nx, nx) * 2 + kap, z * ny + k)

    def leg1_from(s):
        return (lax.rem(x + y - s - 1 + 2 * nx, nx) * 2 + kap, z * ny + s)

    def leg2_to(s):
        return (z, (lax.rem(x + y - s - 1 + 2 * nx, nx) * 2 + kap) * ny + y)

    def leg2_from(s):
        return (lax.rem(lax.div(z, 2) + s - y + 1 + nx, nx) * 2 + lax.rem(z, 2), row * ny + y)

    def leg2_home(s):
        return jnp.logical_and(diag, lax.rem(x + y - s - 1 + 2 * nx, nx) == x)

    def leg2_kept(s):
        return jnp.logical_and(diag, lax.rem(x + s - y + 1 + nx, nx) == x)

    def rows(t):
        return pl.ds(pl.multiple_of(t * tb, tb), tb)

    def lanes(k):
        return pl.ds(pl.multiple_of(k * dc, dc), dc)

    def frows(k):
        return pl.ds(pl.multiple_of(k * fb, fb), fb)

    def rc(src, dst, ss, rs, dev):
        return pltpu.make_async_remote_copy(
            src_ref=src, dst_ref=dst, send_sem=ss, recv_sem=rs,
            device_id=dev, device_id_type=MESH,
        )

    def hcopy(buf, t, ss, rs, dev):
        return rc(buf.at[rows(t)], buf.at[rows(t)], ss, rs, dev)

    def hhalf(buf, t, way, ss, rs, dev):
        ht = tb // 2
        ref = buf.at[pl.ds(pl.multiple_of(t * tb + way * ht, ht), ht)]
        return rc(ref, ref, ss, rs, dev)

    def no(cond):
        return jnp.logical_not(cond)

    loads = [
        pltpu.make_async_copy(src, dst, lsem.at[i])
        for i, (src, dst) in enumerate((
            (tok_hbm, tok),
            (cot_hbm, cot),
            (down_hbm, down),
            (gate_hbm, gw.at[:, pl.ds(0, fb)]),
            (up_hbm, gw.at[:, pl.ds(fb, fb)]),
        ))
    ]
    for load in loads:
        load.start()

    bar = pltpu.get_barrier_semaphore()

    def greet(dev):
        pl.semaphore_signal(bar, inc=1, device_id=dev, device_id_type=MESH)

    greet(mate)
    for d in range(1, nx):
        greet(xdev(d))
    for d in range(1, ny):
        greet(ydev(d))
    for d in range(1, nz):
        greet(zdev(d))

    count = 1 + (nx - 1) + (ny - 1) + (nz - 1) + 2 * ny
    for d in range(nz):
        @pl.when(no(jnp.logical_and(diag, d == 0)))
        def _():
            greet(panel_to(d))

        @pl.when(no(jnp.logical_and(diag, row == d)))
        def _():
            greet(panel_from(d))

        count = count + jnp.where(jnp.logical_and(diag, d == 0), 0, 1)
        count = count + jnp.where(jnp.logical_and(diag, row == d), 0, 1)
    for s in range(ny):
        greet(leg1_to(s))
        greet(leg1_from(s))

        @pl.when(no(leg2_home(s)))
        def _():
            greet(leg2_to(s))

        @pl.when(no(leg2_kept(s)))
        def _():
            greet(leg2_from(s))

        count = count + jnp.where(leg2_home(s), 0, 1) + jnp.where(leg2_kept(s), 0, 1)
    pl.semaphore_wait(bar, count)

    def sub(w, k):
        return lanes(w * ny + k)

    far_first = sorted(range(nz), key=lambda d: -min(d, nz - d))

    def panel_send(w):
        src, ss, sr = ((tok, tos, tor), (cot, cos, cor))[w]
        for d in far_first:
            @pl.when(no(jnp.logical_and(diag, d == 0)))
            def _():
                rc(src, xg.at[rows(row), sub(w, y)], ss.at[d], sr.at[row], panel_to(d)).start()

        @pl.when(diag)
        def _():
            xg[rows(row), sub(w, y)] = src[...]

    def panel_y(w, r, d):
        ss, sr = ((tys, tyr), (cys, cyr))[w]
        ref = xg.at[rows(r), sub(w, y)]
        return rc(ref, ref, ss.at[r, d - 1], sr.at[r, d - 1], ydev(d))

    def panel_pass(w, r):
        sr = (tor, cor)[w]

        @pl.when(no(jnp.logical_and(diag, row == r)))
        def _():
            ref = xg.at[rows(r), sub(w, y)]
            rc(ref, ref, sr.at[r], sr.at[r], panel_from(r)).wait_recv()

        for d in range(1, ny):
            panel_y(w, r, d).start()

    def panel_whole(w, r):
        sr = (tyr, cyr)[w]
        for d in range(1, ny):
            ref = xg.at[rows(r), sub(w, lax.rem(y - d + ny, ny))]
            rc(ref, ref, sr.at[r, d - 1], sr.at[r, d - 1], ydev(d)).wait_recv()

    def order(i):
        return lax.rem(x + 1 + lax.div(i, 2), nx) * 2 + lax.rem(i, 2)

    def leg2(src, dst_of, s1, r1, s2, r2, s):
        ref = src.at[s]
        rc(ref, ref, s1.at[s], r1.at[s], leg1_from(s)).wait_recv()

        @pl.when(no(leg2_home(s)))
        def _():
            rc(ref, dst_of(s), s2.at[s], r2.at[s], leg2_to(s)).start()

        @pl.when(leg2_home(s))
        def _():
            pltpu.make_async_copy(ref, dst_of(s), lsem.at[5]).start()
            pltpu.make_async_copy(ref, dst_of(s), lsem.at[5]).wait()

    def dp_at(s):
        return dp.at[:, lanes(s)]

    def dg_at(s):
        return dg_o.at[frows(s)]

    loads[2].wait()
    for k in range(ny):
        rc(down.at[frows(k)], mid.at[y], d1s.at[k], d1r.at[y], leg1_to(k)).start()

    loads[0].wait()
    panel_send(0)
    loads[1].wait()
    panel_send(1)

    for s in range(ny):
        leg2(mid, dp_at, d1s, d1r, d2s, d2r, s)

    def pass_tok(i, carry):
        panel_pass(0, order(i))
        return carry

    lax.fori_loop(0, nr, pass_tok, 0)
    loads[3].wait()
    loads[4].wait()

    def reduce_pair(t, acc, mr, xs, xr, ms_sem, mr_sem, xs_sem, xr_sem):
        xt = lax.div(t, 2)
        ref = mr.at[xt]
        rc(ref, ref, ms_sem.at[xt], mr_sem.at[xt], mate).wait_recv()

        @pl.when(xt == x)
        def _():
            acc[xt] = acc[xt] + mr[xt]

        @pl.when(xt != x)
        def _():
            d = lax.rem(xt - x + nx, nx)
            xs[d] = (acc[xt] + mr[xt]).astype(BF)
            rc(xs.at[d], xr.at[d], xs_sem.at[d], xr_sem.at[d], xdev(d)).start()

    set_a = (acc_a, mr_a, xs_a, xr_a, mas, mar, xas, xar)
    set_b = (acc_b, mr_b, xs_b, xr_b, mbs, mbr, xbs, xbr)

    def give(t, part, acc, ms, mr, s_sem, r_sem):
        xt = lax.div(t, 2)

        @pl.when(lax.rem(t, 2) == kap)
        def _():
            acc[xt] = part

        @pl.when(lax.rem(t, 2) != kap)
        def _():
            ms[xt] = part
            rc(ms.at[xt], mr.at[xt], s_sem.at[xt], r_sem.at[xt], mate).start()

    def step_a(i, carry):
        t = order(i)
        panel_whole(0, t)
        part = nn(xg[rows(t), pl.ds(0, db)], gw[...])
        give(t, part, acc_a, ms_a, mr_a, mas, mar)

        before = order(jnp.maximum(i - 1, 0))

        @pl.when(jnp.logical_and(i > 0, lax.rem(before, 2) == kap))
        def _():
            reduce_pair(before, *set_a)

        @pl.when(i >= nr // 2)
        def _():
            panel_pass(1, order(2 * i - nr))
            panel_pass(1, order(2 * i - nr + 1))

        return carry

    lax.fori_loop(0, nr, step_a, 0)

    @pl.when(lax.rem(order(nr - 1), 2) == kap)
    def _():
        reduce_pair(order(nr - 1), *set_a)

    chunk = 16

    def spot(i):
        r0 = pl.multiple_of(i * chunk, chunk)
        return pl.ds(r0, chunk), pl.ds(pl.multiple_of(row * tb + r0, chunk), chunk)

    for d in range(1, nx):
        rc(xr_a.at[d], xr_a.at[d], xas.at[d], xar.at[d], xdev(d)).wait_recv()

    def point_h(i, carry):
        here, there = spot(i)
        sa = acc_a[x, here, :]
        for d in range(1, nx):
            sa = sa + xr_a[d, here, :].astype(F32)
        acc_a[x, here, :] = sa
        g, u = sa[:, :fb], sa[:, fb:]
        hh[there, :] = (g * jax.nn.sigmoid(g) * u).astype(BF)
        return carry

    lax.fori_loop(0, tb // chunk, point_h, 0)

    def share(buf, xs_sem, xr_sem, ms_sem, mr_sem):
        for d in near:
            hcopy(buf, row, xs_sem.at[d], xr_sem.at[d], xdev(d)).start()
        hcopy(buf, row, ms_sem.at[0], mr_sem.at[0], mate).start()

    def kin(d):
        return lax.rem(x - d + nx, nx) * 2 + kap

    share(hh, hxs, hxr, hms, hmr)

    for s in range(ny):
        @pl.when(no(leg2_kept(s)))
        def _():
            rc(dp_at(s), dp_at(s), d2s.at[s], d2r.at[s], leg2_from(s)).wait_recv()

    def step_b(i, carry):
        t = order(i)
        panel_whole(1, t)
        part = nt(xg[rows(t), pl.ds(db, db)], dp[...])
        give(t, part, acc_b, ms_b, mr_b, mbs, mbr)

        before = order(jnp.maximum(i - 1, 0))

        @pl.when(jnp.logical_and(i > 0, lax.rem(before, 2) == kap))
        def _():
            reduce_pair(before, *set_b)

        return carry

    lax.fori_loop(0, nr, step_b, 0)

    @pl.when(lax.rem(order(nr - 1), 2) == kap)
    def _():
        reduce_pair(order(nr - 1), *set_b)

    def dist(j):
        q = lax.div(j, 2)
        return jnp.where(lax.rem(q, 2) == 1, lax.div(q + 1, 2), lax.rem(nx - lax.div(q, 2), nx))

    def block(j):
        src = lax.rem(x - dist(j) + nx, nx)
        return src * 2 + jnp.where(lax.rem(j, 2) == 0, kap, 1 - kap)

    def arrive(buf, j, xs_sem, xr_sem, ms_sem, mr_sem):
        t, d = block(j), dist(j)
        even = lax.rem(j, 2) == 0

        @pl.when(j == 2)
        def _():
            for e in near:
                hcopy(buf, kin(e), xs_sem.at[e], xr_sem.at[e], xdev(e)).wait_recv()
                if opposite:
                    way = 0 if e == 1 else 1
                    hhalf(buf, kin(e), way, xs_sem.at[2 + way * (nx - 2)], xr_sem.at[2 + way * (nx - 2)], xdev(e)).start()
            for e in near:
                hcopy(buf, kin(e), ms_sem.at[e], mr_sem.at[e], mate).start()

        if opposite:
            @pl.when(jnp.logical_and(even, d == opposite))
            def _():
                for way in range(2):
                    sem = xr_sem.at[2 + way * (nx - 2)]
                    hhalf(buf, t, way, sem, sem, xdev(1)).wait_recv()
                hcopy(buf, t, ms_sem.at[d], mr_sem.at[d], mate).start()

        @pl.when(no(even))
        def _():
            hcopy(buf, t, ms_sem.at[d], mr_sem.at[d], mate).wait_recv()

    def ycopy(w, t, d):
        os, yr, ss, rs = ((os_o, yr_o, yos, yor), (os_t, yr_t, yts, ytr))[w]
        return rc(os.at[t, d - 1], yr.at[t, d - 1], ss.at[t, d - 1], rs.at[t, d - 1], ydev(d))

    def spread(w, t, part):
        os, own = ((os_o, own_o), (os_t, own_t))[w]
        o32[...] = part
        for e in range(1, ny):
            os[t, e - 1] = o32[:, lanes(lax.rem(y + e, ny))].astype(BF)
            ycopy(w, t, e).start()
        own[t] = o32[:, lanes(y)]

    def zcopy(w, d):
        return rc(zs.at[w, d], zr.at[w, d], zsm.at[w, d], zrm.at[w, d], zdev(d))

    def reduce_y(w, t):
        own, yr = ((own_o, yr_o), (own_t, yr_t))[w]
        total = own[t]
        for d in range(1, ny):
            ycopy(w, t, d).wait_recv()
            total = total + yr[t, d - 1].astype(F32)

        @pl.when(t == z)
        def _():
            zown[w] = total

        @pl.when(t != z)
        def _():
            d = lax.rem(t - z + nz, nz)
            zs[w, d] = total.astype(BF)
            zcopy(w, d).start()

    def step_c(j, carry):
        arrive(hh, j, hxs, hxr, hms, hmr)
        t = block(j)
        spread(0, t, nn(hh[rows(t), :], dp[...]))
        return carry

    lax.fori_loop(0, nr, step_c, 0)

    for k in range(ny):
        dgs[k] = tn(hh[...], xg[:, pl.ds(db + k * dc, dc)]).astype(BF)
        rc(dgs.at[k], mid2.at[y], e1s.at[k], e1r.at[y], leg1_to(k)).start()

    for d in range(1, nx):
        rc(xr_b.at[d], xr_b.at[d], xbs.at[d], xbr.at[d], xdev(d)).wait_recv()

    def point_g(i, carry):
        here, there = spot(i)
        sa = acc_a[x, here, :]
        sb = acc_b[x, here, :]
        for d in range(1, nx):
            sb = sb + xr_b[d, here, :].astype(F32)
        g, u = sa[:, :fb], sa[:, fb:]
        sig = jax.nn.sigmoid(g)
        hg[there, pl.ds(0, fb)] = (sb * u * sig * (1.0 + g * (1.0 - sig))).astype(BF)
        hg[there, pl.ds(fb, fb)] = (sb * (g * sig)).astype(BF)
        return carry

    lax.fori_loop(0, tb // chunk, point_g, 0)
    share(hg, gxs, gxr, gms, gmr)

    for s in range(ny):
        leg2(mid2, dg_at, e1s, e1r, e2s, e2r, s)

    lag = 2

    def step_d(j, carry):
        arrive(hg, j, gxs, gxr, gms, gmr)
        t = block(j)
        spread(1, t, nt(hg[rows(t), :], gw[...]))
        reduce_y(0, t)

        @pl.when(j >= lag)
        def _():
            reduce_y(1, block(jnp.maximum(j - lag, 0)))

        return carry

    lax.fori_loop(0, nr, step_d, 0)

    for k in range(ny):
        w = tn(xg[:, pl.ds(k * dc, dc)], hg[...]).astype(BF)
        gg_o[pl.ds(k * dc, dc)] = w[:, :fb]
        ug_o[pl.ds(k * dc, dc)] = w[:, fb:]

    for j in range(nr - lag, nr):
        reduce_y(1, block(j))

    def fcopy(w):
        return rc(fs.at[w], (out_o, tg_o)[w], f_s.at[w], f_r.at[w], twin)

    for w in range(2):
        total = zown[w]
        for d in range(1, nz):
            zcopy(w, d).wait_recv()
            total = total + zr[w, d].astype(F32)
        fs[w] = total.astype(BF)

        @pl.when(diag)
        def _():
            (out_o, tg_o)[w][...] = fs[w]

        @pl.when(no(diag))
        def _():
            fcopy(w).start()

    @pl.when(no(diag))
    def _():
        for w in range(2):
            fcopy(w).wait_recv()

    for s in range(ny):
        @pl.when(no(leg2_kept(s)))
        def _():
            rc(dg_at(s), dg_at(s), e2s.at[s], e2r.at[s], leg2_from(s)).wait_recv()

    @pl.when(no(diag))
    def _():
        for w in range(2):
            fcopy(w).wait_send()

    for k in range(ny):
        rc(dgs.at[k], mid.at[k], d1s.at[k], d1r.at[k], leg1_to(k)).wait_send()
        rc(dgs.at[k], mid.at[k], e1s.at[k], e1r.at[k], leg1_to(k)).wait_send()

        @pl.when(no(leg2_home(k)))
        def _():
            rc(mid.at[k], dp_at(k), d2s.at[k], d2r.at[k], leg2_to(k)).wait_send()
            rc(mid2.at[k], dg_at(k), e2s.at[k], e2r.at[k], leg2_to(k)).wait_send()

    for d in range(nz):
        @pl.when(no(jnp.logical_and(diag, d == 0)))
        def _():
            rc(tok, tok, tos.at[d], tor.at[d], panel_to(d)).wait_send()
            rc(cot, cot, cos.at[d], cor.at[d], panel_to(d)).wait_send()

    for q in range(nx):
        rc(ms_a.at[q], mr_a.at[q], mas.at[q], mar.at[q], mate).wait_send()
        rc(ms_b.at[q], mr_b.at[q], mbs.at[q], mbr.at[q], mate).wait_send()
        hcopy(hh, row, hms.at[q], hmr.at[q], mate).wait_send()
        hcopy(hg, row, gms.at[q], gmr.at[q], mate).wait_send()
    for d in range(1, nx):
        rc(xs_a.at[d], xr_a.at[d], xas.at[d], xar.at[d], xdev(d)).wait_send()
        rc(xs_b.at[d], xr_b.at[d], xbs.at[d], xbr.at[d], xdev(d)).wait_send()
    for d in near:
        hcopy(hh, row, hxs.at[d], hxr.at[d], xdev(d)).wait_send()
        hcopy(hg, row, gxs.at[d], gxr.at[d], xdev(d)).wait_send()
    if opposite:
        for e in (2, nx):
            hhalf(hh, row, 0, hxs.at[e], hxr.at[e], xdev(1)).wait_send()
            hhalf(hg, row, 0, gxs.at[e], gxr.at[e], xdev(1)).wait_send()
    for d in range(1, nz):
        zcopy(0, d).wait_send()
        zcopy(1, d).wait_send()

    def ydone(t, carry):
        for d in range(1, ny):
            panel_y(0, t, d).wait_send()
            panel_y(1, t, d).wait_send()
            ycopy(0, t, d).wait_send()
            ycopy(1, t, d).wait_send()
        return carry

    lax.fori_loop(0, nr, ydone, 0)


def local(dims, tokens, gate_weight, up_weight, down_weight, out_grad):
    nx, ny, nz = dims
    nr = 2 * nx
    tb, dc = tokens.shape
    db, fb = gate_weight.shape
    t = nr * tb
    vm = pl.BlockSpec(memory_space=pltpu.VMEM)
    hbm = pl.BlockSpec(memory_space=pl.ANY)
    dma = pltpu.SemaphoreType.DMA

    def sums(width):
        return [
            pltpu.VMEM((nx, tb, width), F32),
            pltpu.VMEM((nx, tb, width), F32),
            pltpu.VMEM((nx, tb, width), F32),
            pltpu.VMEM((nx, tb, width), BF),
            pltpu.VMEM((nx, tb, width), BF),
        ]

    def shares():
        return [
            pltpu.VMEM((nr, ny - 1, tb, dc), BF),
            pltpu.VMEM((nr, tb, dc), F32),
            pltpu.VMEM((nr, ny - 1, tb, dc), BF),
        ]

    scratch = [
        pltpu.VMEM((tb, dc), BF),
        pltpu.VMEM((tb, dc), BF),
        pltpu.VMEM((ny * fb, dc), BF),
        pltpu.VMEM((t, 2 * db), BF),
        pltpu.VMEM((db, 2 * fb), BF),
        pltpu.VMEM((fb, db), BF),
        pltpu.VMEM((t, fb), BF),
        pltpu.VMEM((t, 2 * fb), BF),
        pltpu.VMEM((ny, fb, dc), BF),
        pltpu.VMEM((ny, fb, dc), BF),
        *sums(2 * fb),
        *sums(fb),
        pltpu.VMEM((tb, db), F32),
        *shares(),
        *shares(),
        pltpu.VMEM((2, nz, tb, dc), BF),
        pltpu.VMEM((2, nz, tb, dc), BF),
        pltpu.VMEM((2, tb, dc), F32),
        pltpu.VMEM((2, tb, dc), BF),
        pltpu.VMEM((ny, fb, dc), BF),
        dma((nz,)), dma((nr,)), dma((nz,)), dma((nr,)),
        *[dma((nr, ny - 1))] * 4,
        *[dma((ny,))] * 8,
        *[dma((nx,))] * 8,
        *[dma((nx + 1,))] * 8,
        *[dma((nr, ny - 1))] * 4,
        dma((2, nz)), dma((2, nz)), dma((2,)), dma((2,)), dma((6,)),
    ]
    shape = jax.ShapeDtypeStruct
    return pl.pallas_call(
        functools.partial(kernel, dims),
        out_shape=(
            shape((tb, dc), BF),
            shape((tb, dc), BF),
            shape((db, fb), BF),
            shape((db, fb), BF),
            shape((ny * fb, dc), BF),
        ),
        in_specs=[hbm] * 5,
        out_specs=(vm,) * 5,
        scratch_shapes=scratch,
        compiler_params=pltpu.CompilerParams(
            collective_id=0, has_side_effects=True, vmem_limit_bytes=60 * 2**20
        ),
        name="swiglu",
    )(tokens, out_grad, gate_weight, up_weight, down_weight)


def solution(mesh):
    nr, nc = mesh.shape["row"], mesh.shape["col"]
    dims = (nr // 2, nc // nr, nr)
    spec = P("row", "col")
    return jax.shard_map(
        functools.partial(local, dims),
        mesh=mesh,
        in_specs=(spec,) * 5,
        out_specs=(spec,) * 5,
        check_vma=False,
    )
```

time: 138 us -> 117 us (0.85)
  Pallas kernels: 128 us -> 110 us
  local copies, waits for them, and re-layouts: 8.24 us -> 5.95 us
    pallas_call x1, Pallas kernels: 128 us -> 110 us  [local(): pl.pallas_call(functools.partial(kernel, dims), out_shape=(shape((tb, dc)...]
    unnamed x15 -> x11, local copies, waits for them, and re-layouts: 8.24 us -> 5.95 us
where the time goes in v3:
time: 117 us; the launch traced here: 116 us
  Pallas kernels  110 us (94%)
  local copies, waits for them, and re-layouts  5.95 us (5%)
    pallas_call x1, Pallas kernels, local(): pl.pallas_call(functools.partial(kernel, dims), out_shape=(shape((tb, dc)...  110 us
    unnamed x11, local copies, waits for them, and re-layouts  5.95 us

profile of v3, /device:TPU:4, one launch (start us, length us, event | category | flops | bytes accessed | tf_op | source)
XLA Modules:
  0.0 116.4 jit_solution(8798006332977771897)
XLA Ops:
  0.6 109.8 %swiglu.1 = (bf16[128,128]{1,0:T(8,128)(2,1)}, bf16[128,128]{1,0:T(8,128)(2,1)}, bf16[512,512]{1,0:T(8,128)(2,1)}, bf16[512,512]{1,0:T(8,128)(2,1)}, bf16[2048,128]{1,0:T(8,128)(2,1)}) custom-call(bf16[128,128]{1,0:T(8,128)(2,1)} %tok_hbm.1, bf16[128,128]{1,0:T(8,128)(2,1)} %cot_hbm.1, bf16[512,512]{1,0:T(8,128)(2,1)} %gate_hbm.1, bf16[512,512]{1,0:T(8,128)(2,1)} %up_hbm.1, ...), custom_call_target="tpu_custom_call" | custom-call | tf_op jit(solution)/shard_map/swiglu/pallas_call | solution.py:617
  110.4 0.0 copy-start.2
  110.4 1.4 %copy.15 = bf16[128,128]{1,0:T(8,128)(2,1)} copy(bf16[128,128]{1,0:T(8,128)(2,1)} %get-tuple-element.10) | data formatting | bytes 65536
  111.8 0.0 copy-done.2
  111.8 0.6 copy.16
  112.4 0.0 copy-start.1
  112.4 1.9 %copy.17 = bf16[512,512]{1,0:T(8,128)(2,1)} copy(bf16[512,512]{1,0:T(8,128)(2,1)} %get-tuple-element.12) | data formatting | bytes 1048576
  114.4 0.0 copy-done.1
  114.4 0.0 copy-start
  114.4 0.8 copy.18
  115.2 0.4 copy-done
  115.6 0.8 copy.19
Async XLA Ops:
  110.4 1.4 %copy-start.2 = (bf16[128,128]{1,0:T(8,128)(2,1)S(1)}, bf16[128,128]{1,0:T(8,128)(2,1)}, u32[]{:S(2)}) copy-start(bf16[128,128]{1,0:T(8,128)(2,1)} %get-tuple-element.11) | copy-start | bytes 98308
  112.4 1.9 %copy-start.1 = (bf16[512,512]{1,0:T(8,128)(2,1)S(1)}, bf16[512,512]{1,0:T(8,128)(2,1)}, u32[]{:S(2)}) copy-start(bf16[512,512]{1,0:T(8,128)(2,1)} %get-tuple-element.13) | copy-start | bytes 1572868
  114.4 1.2 %copy-start = (bf16[2048,128]{1,0:T(8,128)(2,1)S(1)}, bf16[2048,128]{1,0:T(8,128)(2,1)}, u32[]{:S(2)}) copy-start(bf16[2048,128]{1,0:T(8,128)(2,1)} %get-tuple-element.14) | copy-start | bytes 1572868

commit v4 on v3

--- a/solution.py
+++ b/solution.py
@@ -32,7 +32,7 @@
     acc_a, ms_a, mr_a, xs_a, xr_a,
     acc_b, ms_b, mr_b, xs_b, xr_b,
     o32, os_o, own_o, yr_o, os_t, own_t, yr_t,
-    zs, zr, zown, fs, dgs,
+    zs, zr, zown, fs, dgs, wgs,
     tos, tor, cos, cor, tys, tyr, cys, cyr,
     d1s, d1r, d2s, d2r, e1s, e1r, e2s, e2r,
     mas, mar, mbs, mbr, xas, xar, xbs, xbr,
@@ -53,6 +53,9 @@
 
     near = sorted({1, nx - 1})
     opposite = nx // 2 if nx > 2 else 0
+
+    near_y = sorted({1, ny - 1})
+    far_y = ny // 2 if ny > 2 else 0
 
     def xdev(d):
         return (lax.rem(x + d, nx) * 2 + kap, col)
@@ -195,14 +198,29 @@
             ref = xg.at[rows(r), sub(w, y)]
             rc(ref, ref, sr.at[r], sr.at[r], panel_from(r)).wait_recv()
 
-        for d in range(1, ny):
+        for d in near_y:
             panel_y(w, r, d).start()
 
+    def panel_from_y(w, r, d, dev):
+        ss, sr = ((tys, tyr), (cys, cyr))[w]
+        ref = xg.at[rows(r), sub(w, lax.rem(y - d + ny, ny))]
+        return rc(ref, ref, ss.at[r, d - 1], sr.at[r, d - 1], dev)
+
+    def panel_next(w, r):
+        for d in near_y:
+            panel_from_y(w, r, d, ydev(d)).wait_recv()
+        if far_y:
+            sr = (tyr, cyr)[w]
+            ss = (tys, cys)[w]
+            for side, d in enumerate(near_y):
+                @pl.when(lax.rem(r, 2) == side)
+                def _():
+                    ref = xg.at[rows(r), sub(w, lax.rem(y - d + ny, ny))]
+                    rc(ref, ref, ss.at[r, far_y - 1], sr.at[r, far_y - 1], ydev(d)).start()
+
     def panel_whole(w, r):
-        sr = (tyr, cyr)[w]
-        for d in range(1, ny):
-            ref = xg.at[rows(r), sub(w, lax.rem(y - d + ny, ny))]
-            rc(ref, ref, sr.at[r, d - 1], sr.at[r, d - 1], ydev(d)).wait_recv()
+        if far_y:
+            panel_from_y(w, r, far_y, ydev(1)).wait_recv()
 
     def order(i):
         return lax.rem(x + 1 + lax.div(i, 2), nx) * 2 + lax.rem(i, 2)
@@ -226,17 +244,14 @@
     def dg_at(s):
         return dg_o.at[frows(s)]
 
+    loads[0].wait()
+    panel_send(0)
     loads[2].wait()
     for k in range(ny):
         rc(down.at[frows(k)], mid.at[y], d1s.at[k], d1r.at[y], leg1_to(k)).start()
 
-    loads[0].wait()
-    panel_send(0)
     loads[1].wait()
     panel_send(1)
-
-    for s in range(ny):
-        leg2(mid, dp_at, d1s, d1r, d2s, d2r, s)
 
     def pass_tok(i, carry):
         panel_pass(0, order(i))
@@ -276,8 +291,20 @@
             ms[xt] = part
             rc(ms.at[xt], mr.at[xt], s_sem.at[xt], r_sem.at[xt], mate).start()
 
+    for s in range(ny):
+        leg2(mid, dp_at, d1s, d1r, d2s, d2r, s)
+
+    ahead = 2
+    for i in range(ahead):
+        panel_next(0, order(i))
+
     def step_a(i, carry):
         t = order(i)
+
+        @pl.when(i + ahead < nr)
+        def _():
+            panel_next(0, order(i + ahead))
+
         panel_whole(0, t)
         part = nn(xg[rows(t), pl.ds(0, db)], gw[...])
         give(t, part, acc_a, ms_a, mr_a, mas, mar)
@@ -300,6 +327,12 @@
     @pl.when(lax.rem(order(nr - 1), 2) == kap)
     def _():
         reduce_pair(order(nr - 1), *set_a)
+
+    def next_cot(i, carry):
+        panel_next(1, order(i))
+        return carry
+
+    lax.fori_loop(0, nr, next_cot, 0)
 
     chunk = 16
 
@@ -472,13 +505,19 @@
 
     lax.fori_loop(0, nr, step_d, 0)
 
+    for j in range(nr - lag, nr):
+        reduce_y(1, block(j))
+
     for k in range(ny):
         w = tn(xg[:, pl.ds(k * dc, dc)], hg[...]).astype(BF)
-        gg_o[pl.ds(k * dc, dc)] = w[:, :fb]
-        ug_o[pl.ds(k * dc, dc)] = w[:, fb:]
-
-    for j in range(nr - lag, nr):
-        reduce_y(1, block(j))
+        wgs[pl.ds(k * dc, dc)] = w
+
+    grads = [
+        pltpu.make_async_copy(wgs.at[:, pl.ds(i * fb, fb)], dst, lsem.at[i])
+        for i, dst in enumerate((gg_o, ug_o))
+    ]
+    for copy in grads:
+        copy.start()
 
     def fcopy(w):
         return rc(fs.at[w], (out_o, tg_o)[w], f_s.at[w], f_r.at[w], twin)
@@ -492,7 +531,9 @@
 
         @pl.when(diag)
         def _():
-            (out_o, tg_o)[w][...] = fs[w]
+            kept = pltpu.make_async_copy(fs.at[w], (out_o, tg_o)[w], lsem.at[5])
+            kept.start()
+            kept.wait()
 
         @pl.when(no(diag))
         def _():
@@ -507,6 +548,9 @@
         @pl.when(no(leg2_kept(s)))
         def _():
             rc(dg_at(s), dg_at(s), e2s.at[s], e2r.at[s], leg2_from(s)).wait_recv()
+
+    for copy in grads:
+        copy.wait()
 
     @pl.when(no(diag))
     def _():
@@ -558,13 +602,24 @@
     lax.fori_loop(0, nr, ydone, 0)
 
 
+def place(*refs):
+    sems = refs[-1]
+    copies = [
+        pltpu.make_async_copy(src, dst, sems.at[i])
+        for i, (src, dst) in enumerate(zip(refs[:5], refs[5:10]))
+    ]
+    for copy in copies:
+        copy.start()
+    for copy in copies:
+        copy.wait()
+
+
 def local(dims, tokens, gate_weight, up_weight, down_weight, out_grad):
     nx, ny, nz = dims
     nr = 2 * nx
     tb, dc = tokens.shape
     db, fb = gate_weight.shape
     t = nr * tb
-    vm = pl.BlockSpec(memory_space=pltpu.VMEM)
     hbm = pl.BlockSpec(memory_space=pl.ANY)
     dma = pltpu.SemaphoreType.DMA
 
@@ -605,6 +660,7 @@
         pltpu.VMEM((2, tb, dc), F32),
         pltpu.VMEM((2, tb, dc), BF),
         pltpu.VMEM((ny, fb, dc), BF),
+        pltpu.VMEM((db, 2 * fb), BF),
         dma((nz,)), dma((nr,)), dma((nz,)), dma((nr,)),
         *[dma((nr, ny - 1))] * 4,
         *[dma((ny,))] * 8,
@@ -614,23 +670,33 @@
         dma((2, nz)), dma((2, nz)), dma((2,)), dma((2,)), dma((6,)),
     ]
     shape = jax.ShapeDtypeStruct
-    return pl.pallas_call(
+    results = (
+        shape((tb, dc), BF),
+        shape((tb, dc), BF),
+        shape((db, fb), BF),
+        shape((db, fb), BF),
+        shape((ny * fb, dc), BF),
+    )
+    held = pl.pallas_call(
         functools.partial(kernel, dims),
-        out_shape=(
-            shape((tb, dc), BF),
-            shape((tb, dc), BF),
-            shape((db, fb), BF),
-            shape((db, fb), BF),
-            shape((ny * fb, dc), BF),
-        ),
+        out_shape=results,
         in_specs=[hbm] * 5,
-        out_specs=(vm,) * 5,
+        out_specs=(hbm,) * 5,
         scratch_shapes=scratch,
         compiler_params=pltpu.CompilerParams(
             collective_id=0, has_side_effects=True, vmem_limit_bytes=60 * 2**20
         ),
         name="swiglu",
     )(tokens, out_grad, gate_weight, up_weight, down_weight)
+    return pl.pallas_call(
+        place,
+        out_shape=results,
+        in_specs=[pl.BlockSpec(memory_space=pltpu.VMEM)] * 5,
+        out_specs=(hbm,) * 5,
+        scratch_shapes=[dma((5,))],
+        compiler_params=pltpu.CompilerParams(has_side_effects=True),
+        name="place",
+    )(*held)
 
 
 def solution(mesh):

time: 117 us -> 112 us (0.957)
  local copies, waits for them, and re-layouts: 5.95 us -> 0 us
    unnamed x11 -> x0, local copies, waits for them, and re-layouts: 5.95 us -> none
    pallas_call x1 -> x2, Pallas kernels: 110 us -> 111 us  [the longest x1 109 us: local(): pl.pallas_call(functools.partial(kernel, dims), out_shape=results, in_spe...]
where the time goes in v4:
time: 112 us
  Pallas kernels  111 us (99%)
    pallas_call x1, Pallas kernels, local(): pl.pallas_call(functools.partial(kernel, dims), out_shape=results, in_spe...  109 us
    pallas_call x1, Pallas kernels, local(): pl.pallas_call(place, out_shape=results, in_specs=[pl.BlockSpec(memory_sp...  2.6 us

profile of v4, /device:TPU:4, one launch (start us, length us, event | category | flops | bytes accessed | tf_op | source)
XLA Modules:
  0.0 112.0 jit_solution(1203996555703416859)
XLA Ops:
  0.6 108.8 %swiglu.1 = (bf16[128,128]{1,0:T(8,128)(2,1)}, bf16[128,128]{1,0:T(8,128)(2,1)}, bf16[512,512]{1,0:T(8,128)(2,1)}, bf16[512,512]{1,0:T(8,128)(2,1)}, bf16[2048,128]{1,0:T(8,128)(2,1)}) custom-call(bf16[128,128]{1,0:T(8,128)(2,1)} %tok_hbm.1, bf16[128,128]{1,0:T(8,128)(2,1)} %cot_hbm.1, bf16[512,512]{1,0:T(8,128)(2,1)} %gate_hbm.1, bf16[512,512]{1,0:T(8,128)(2,1)} %up_hbm.1, ...), custom_call_target="tpu_custom_call" | custom-call | tf_op jit(solution)/shard_map/swiglu/pallas_call | solution.py:680
  109.4 2.6 %place.1 = (bf16[128,128]{1,0:T(8,128)(2,1)}, bf16[128,128]{1,0:T(8,128)(2,1)}, bf16[512,512]{1,0:T(8,128)(2,1)}, bf16[512,512]{1,0:T(8,128)(2,1)}, bf16[2048,128]{1,0:T(8,128)(2,1)}) custom-call(bf16[128,128]{1,0:T(8,128)(2,1)} %get-tuple-element.10.refs_0_, bf16[128,128]{1,0:T(8,128)(2,1)} %get-tuple-element.11.refs_1_, ...), custom_call_target="tpu_custom_call" | custom-call | tf_op jit(solution)/shard_map/place/pallas_call | solution.py:691

commit v5 on v4

--- a/solution.py
+++ b/solution.py
@@ -244,12 +244,12 @@
     def dg_at(s):
         return dg_o.at[frows(s)]
 
-    loads[0].wait()
-    panel_send(0)
     loads[2].wait()
     for k in range(ny):
         rc(down.at[frows(k)], mid.at[y], d1s.at[k], d1r.at[y], leg1_to(k)).start()
 
+    loads[0].wait()
+    panel_send(0)
     loads[1].wait()
     panel_send(1)
 
@@ -486,6 +486,12 @@
     lax.fori_loop(0, tb // chunk, point_g, 0)
     share(hg, gxs, gxr, gms, gmr)
 
+    def sum_o(j, carry):
+        reduce_y(0, block(j))
+        return carry
+
+    lax.fori_loop(0, nr, sum_o, 0)
+
     for s in range(ny):
         leg2(mid2, dg_at, e1s, e1r, e2s, e2r, s)
 
@@ -495,8 +501,6 @@
         arrive(hg, j, gxs, gxr, gms, gmr)
         t = block(j)
         spread(1, t, nt(hg[rows(t), :], gw[...]))
-        reduce_y(0, t)
-
         @pl.when(j >= lag)
         def _():
             reduce_y(1, block(jnp.maximum(j - lag, 0)))

time: 112 us -> 112 us (level)
  no operation moved by 1% of the time
where the time goes in v5:
time: 112 us; the launch traced here: 111 us
  Pallas kernels  110 us (98%)
    pallas_call x1, Pallas kernels, local(): pl.pallas_call(functools.partial(kernel, dims), out_shape=results, in_spe...  108 us
    pallas_call x1, Pallas kernels, local(): pl.pallas_call(place, out_shape=results, in_specs=[pl.BlockSpec(memory_sp...  2.6 us

profile of v5, /device:TPU:4, one launch (start us, length us, event | category | flops | bytes accessed | tf_op | source)
XLA Modules:
  0.0 111.1 jit_solution(2831385586980501179)
XLA Ops:
  0.6 107.8 %swiglu.1 = (bf16[128,128]{1,0:T(8,128)(2,1)}, bf16[128,128]{1,0:T(8,128)(2,1)}, bf16[512,512]{1,0:T(8,128)(2,1)}, bf16[512,512]{1,0:T(8,128)(2,1)}, bf16[2048,128]{1,0:T(8,128)(2,1)}) custom-call(bf16[128,128]{1,0:T(8,128)(2,1)} %tok_hbm.1, bf16[128,128]{1,0:T(8,128)(2,1)} %cot_hbm.1, bf16[512,512]{1,0:T(8,128)(2,1)} %gate_hbm.1, bf16[512,512]{1,0:T(8,128)(2,1)} %up_hbm.1, ...), custom_call_target="tpu_custom_call" | custom-call | tf_op jit(solution)/shard_map/swiglu/pallas_call | solution.py:684
  108.5 2.6 %place.1 = (bf16[128,128]{1,0:T(8,128)(2,1)}, bf16[128,128]{1,0:T(8,128)(2,1)}, bf16[512,512]{1,0:T(8,128)(2,1)}, bf16[512,512]{1,0:T(8,128)(2,1)}, bf16[2048,128]{1,0:T(8,128)(2,1)}) custom-call(bf16[128,128]{1,0:T(8,128)(2,1)} %get-tuple-element.10.refs_0_, bf16[128,128]{1,0:T(8,128)(2,1)} %get-tuple-element.11.refs_1_, ...), custom_call_target="tpu_custom_call" | custom-call | tf_op jit(solution)/shard_map/place/pallas_call | solution.py:695

commit v6 on v5

--- a/solution.py
+++ b/solution.py
@@ -51,8 +51,7 @@
     diag = row == z
     twin = (z, row * ny + y)
 
-    near = sorted({1, nx - 1})
-    opposite = nx // 2 if nx > 2 else 0
+    near = list(range(1, nx))
 
     near_y = sorted({1, ny - 1})
     far_y = ny // 2 if ny > 2 else 0
@@ -107,11 +106,6 @@
 
     def hcopy(buf, t, ss, rs, dev):
         return rc(buf.at[rows(t)], buf.at[rows(t)], ss, rs, dev)
-
-    def hhalf(buf, t, way, ss, rs, dev):
-        ht = tb // 2
-        ref = buf.at[pl.ds(pl.multiple_of(t * tb + way * ht, ht), ht)]
-        return rc(ref, ref, ss, rs, dev)
 
     def no(cond):
         return jnp.logical_not(cond)
@@ -402,23 +396,10 @@
         t, d = block(j), dist(j)
         even = lax.rem(j, 2) == 0
 
-        @pl.when(j == 2)
-        def _():
-            for e in near:
-                hcopy(buf, kin(e), xs_sem.at[e], xr_sem.at[e], xdev(e)).wait_recv()
-                if opposite:
-                    way = 0 if e == 1 else 1
-                    hhalf(buf, kin(e), way, xs_sem.at[2 + way * (nx - 2)], xr_sem.at[2 + way * (nx - 2)], xdev(e)).start()
-            for e in near:
-                hcopy(buf, kin(e), ms_sem.at[e], mr_sem.at[e], mate).start()
-
-        if opposite:
-            @pl.when(jnp.logical_and(even, d == opposite))
-            def _():
-                for way in range(2):
-                    sem = xr_sem.at[2 + way * (nx - 2)]
-                    hhalf(buf, t, way, sem, sem, xdev(1)).wait_recv()
-                hcopy(buf, t, ms_sem.at[d], mr_sem.at[d], mate).start()
+        @pl.when(jnp.logical_and(even, d > 0))
+        def _():
+            hcopy(buf, t, xs_sem.at[d], xr_sem.at[d], xdev(d)).wait_recv()
+            hcopy(buf, t, ms_sem.at[d], mr_sem.at[d], mate).start()
 
         @pl.when(no(even))
         def _():
@@ -587,10 +568,6 @@
     for d in near:
         hcopy(hh, row, hxs.at[d], hxr.at[d], xdev(d)).wait_send()
         hcopy(hg, row, gxs.at[d], gxr.at[d], xdev(d)).wait_send()
-    if opposite:
-        for e in (2, nx):
-            hhalf(hh, row, 0, hxs.at[e], hxr.at[e], xdev(1)).wait_send()
-            hhalf(hg, row, 0, gxs.at[e], gxr.at[e], xdev(1)).wait_send()
     for d in range(1, nz):
         zcopy(0, d).wait_send()
         zcopy(1, d).wait_send()

time: 112 us -> 112 us (level)
  no operation moved by 1% of the time
where the time goes in v6:
time: 112 us
  Pallas kernels  111 us (99%)
    pallas_call x1, Pallas kernels, local(): pl.pallas_call(functools.partial(kernel, dims), out_shape=results, in_spe...  109 us
    pallas_call x1, Pallas kernels, local(): pl.pallas_call(place, out_shape=results, in_specs=[pl.BlockSpec(memory_sp...  2.6 us

profile of v6, /device:TPU:4, one launch (start us, length us, event | category | flops | bytes accessed | tf_op | source)
XLA Modules:
  0.0 111.9 jit_solution(2662595358321408689)
XLA Ops:
  0.6 108.7 %swiglu.1 = (bf16[128,128]{1,0:T(8,128)(2,1)}, bf16[128,128]{1,0:T(8,128)(2,1)}, bf16[512,512]{1,0:T(8,128)(2,1)}, bf16[512,512]{1,0:T(8,128)(2,1)}, bf16[2048,128]{1,0:T(8,128)(2,1)}) custom-call(bf16[128,128]{1,0:T(8,128)(2,1)} %tok_hbm.1, bf16[128,128]{1,0:T(8,128)(2,1)} %cot_hbm.1, bf16[512,512]{1,0:T(8,128)(2,1)} %gate_hbm.1, bf16[512,512]{1,0:T(8,128)(2,1)} %up_hbm.1, ...), custom_call_target="tpu_custom_call" | custom-call | tf_op jit(solution)/shard_map/swiglu/pallas_call | solution.py:661
  109.3 2.6 %place.1 = (bf16[128,128]{1,0:T(8,128)(2,1)}, bf16[128,128]{1,0:T(8,128)(2,1)}, bf16[512,512]{1,0:T(8,128)(2,1)}, bf16[512,512]{1,0:T(8,128)(2,1)}, bf16[2048,128]{1,0:T(8,128)(2,1)}) custom-call(bf16[128,128]{1,0:T(8,128)(2,1)} %get-tuple-element.10.refs_0_, bf16[128,128]{1,0:T(8,128)(2,1)} %get-tuple-element.11.refs_1_, ...), custom_call_target="tpu_custom_call" | custom-call | tf_op jit(solution)/shard_map/place/pallas_call | solution.py:672
